TPU v7x, 256 devices: a whole 4x4x8 slice. The times are simulated.
256 devices in a mesh: feat: 8 (over z), node: 32 (over x, y, core).
Axes of the slice: x: 4, y: 4, z: 8, core: 2. Of those that a mesh axis runs over, the one named last changes fastest.
Arguments:
- features: bfloat16 [32, 128, 8192], P('node', 'feat'), may hold values from -6 to 6
- tile_columns: int32 [32, 64, 8], P('node'), may hold values from 0 to 2047, as said below
- tile_count: int32 [32, 64], P('node'), may hold values from 1 to 8, as said below
- tile_bits: int32 [32, 64, 8, 2048], P('node'), may hold values from 0 to 255
- labels: int32 [32, 8192], P('node', 'feat'), may hold values from 0 to 171
- train_mask: int32 [32, 8192], P('node', 'feat'), may hold values from 0 to 1
- first_self: bfloat16 [128, 256], replicated, may hold values from -0.5 to 0.5
- first_neighbor: bfloat16 [128, 256], replicated, may hold values from -1.0546875 to 1.0546875
- first_bias: float32 [256], replicated, may hold values from -3 to 3
- second_self: bfloat16 [256, 172], replicated, may hold values from -1.125 to 1.125
- second_neighbor: bfloat16 [256, 172], replicated, may hold values from -1.125 to 1.125
- second_bias: float32 [172], replicated, may hold values from -4 to 4
Outputs:
- logits: float32 [32, 8192, 172], P('node', 'feat')
- loss: float32 [], replicated
- grad_self: float32 [256, 172], replicated
- grad_neighbor: float32 [256, 172], replicated
- grad_bias: float32 [172], replicated
Inputs may be any that keep to these rules, and one draw needn't show every extreme that they name: `tile_columns`: column tiles are numbered over all 262144 nodes; every column tile of a row tile of block b lies in block b - 1, b or b + 1, and slot 0 of each row tile is the row tile itself. `tile_count`: slots at or after the count are ignored.
All inputs are finite; a program needn't handle non-finite values.
Results may differ from a plain program's by a relative error of at most 0.0008.
The roundings to bfloat16 on the way count: a program that leaves them out, or rounds other values in their place, can miss the bound.
Values may be sent and summed in bfloat16 or wider, within the bound.
A program may use at most 128 MiB of HBM per device.

v0:
```python
import math

import jax
import jax.numpy as jnp
from jax import lax
from jax.sharding import PartitionSpec as P


def with_halo(value, sides, width):
    for axis, dim in sides:
        size, length = (lax.axis_size(axis), value.shape[dim])
        up = [(i, (i + 1) % size) for i in range(size - 1)]
        down = [(j, i) for i, j in up]
        last = lax.slice_in_dim(value, length - width, length, axis=dim)
        initial = lax.slice_in_dim(value, 0, width, axis=dim)
        before = lax.ppermute(last, axis, up)
        after = lax.ppermute(initial, axis, down)
        value = jnp.concatenate([before, value, after], axis=dim)
    return value


def unpack_bits(bit_words):
    shifts = jnp.arange(8, dtype=jnp.int32)
    rows = bit_words.reshape(bit_words.shape[:-1] + (128, 16))
    bit_table = jnp.bitwise_and(jnp.right_shift(rows[..., None], shifts), 1)
    return bit_table.reshape(rows.shape[:-1] + (128,))


def aggregate(table, columns, counts, bit_words, pattern):
    picked = jnp.take(table, columns, axis=0)
    slot_valid = (lax.broadcasted_iota(jnp.int32, columns.shape, 1) < counts[:, None]).astype(
        jnp.int32
    )
    bit_table = unpack_bits(bit_words) * slot_valid[:, :, None, None]
    degree = jnp.sum(bit_table, axis=(1, 3)).astype(jnp.float32)
    row_sums = jnp.einsum(
        pattern, bit_table.astype(jnp.bfloat16), picked, preferred_element_type=jnp.float32
    )
    mean_rows = row_sums / jnp.maximum(degree, 1.0)[..., None]
    return mean_rows.reshape(-1, row_sums.shape[-1]).astype(jnp.bfloat16)


def column_tiles(nearby):
    width = nearby.shape[1]
    grouped = nearby.reshape(nearby.shape[0], width, -1, 128)
    return jnp.transpose(grouped, (0, 2, 1, 3)).reshape(-1, width, 128)


def shards(
    features,
    tile_columns,
    tile_count,
    tile_bits,
    labels,
    train_mask,
    first_self,
    first_neighbor,
    first_bias,
    second_self,
    second_neighbor,
    second_bias,
):
    feat_index = lax.axis_index("feat")
    node_index = lax.axis_index("node")
    node_count = lax.axis_size("node")
    block_rows = features.shape[2]
    fine_rows = labels.shape[1]
    fine_tiles = fine_rows // 128
    block_tiles = block_rows // 128
    node_total = block_rows * node_count
    local_columns = tile_columns[0] - (node_index - 1) * block_tiles
    fine_start = feat_index * fine_tiles
    own_columns = lax.dynamic_slice_in_dim(local_columns, fine_start, fine_tiles, 0)
    own_counts = lax.dynamic_slice_in_dim(tile_count[0], fine_start, fine_tiles, 0)
    own_words = lax.dynamic_slice_in_dim(tile_bits[0], fine_start, fine_tiles, 0)
    contract = (((0,), (0,)), ((), ()))
    pattern_split = "tsij,tswj->tiw"
    full_width = lax.all_gather(features, "feat", axis=1, tiled=True)
    nearby = with_halo(full_width, (("node", 0),), 1)
    near_tiles = column_tiles(nearby)
    mean_rows = aggregate(near_tiles, own_columns, own_counts, own_words, pattern_split)
    own_rows = lax.dynamic_slice_in_dim(full_width[0], feat_index * fine_rows, fine_rows, 1)
    preact = lax.dot_general(
        own_rows, first_self, contract, preferred_element_type=jnp.float32
    ) + jnp.dot(mean_rows, first_neighbor, preferred_element_type=jnp.float32)
    hidden = jnp.maximum(preact + first_bias, 0.0).astype(jnp.bfloat16)
    block_hidden = lax.all_gather(hidden, "feat", axis=0, tiled=True)
    near_hidden = with_halo(block_hidden[None], (("node", 0),), 1)
    hidden_tiles = near_hidden.reshape(-1, 128, hidden.shape[1])
    mean_hidden = aggregate(hidden_tiles, own_columns, own_counts, own_words, "tsij,tsjw->tiw")
    logits = (
        jnp.dot(hidden, second_self, preferred_element_type=jnp.float32)
        + jnp.dot(mean_hidden, second_neighbor, preferred_element_type=jnp.float32)
        + second_bias
    )
    exponent = jnp.exp(logits)
    class_total = jnp.sum(exponent, axis=1)
    classes = lax.broadcasted_iota(jnp.int32, logits.shape, 1)
    onehot = (classes == labels[0][:, None]).astype(jnp.float32)
    weight = train_mask[0].astype(jnp.float32)
    row_loss = (jnp.log(class_total) - jnp.sum(onehot * logits, axis=1)) * weight
    grad_scale = 1.0 / math.sqrt(node_total)
    output_grad = (
        (exponent / class_total[:, None] - onehot) * weight[:, None] * grad_scale
    ).astype(jnp.bfloat16)
    grad_self = lax.dot_general(hidden, output_grad, contract, preferred_element_type=jnp.float32)
    grad_neighbor = lax.dot_general(
        mean_hidden, output_grad, contract, preferred_element_type=jnp.float32
    )
    grad_bias = jnp.sum(output_grad.astype(jnp.float32), axis=0)
    loss_part = jnp.sum(row_loss) / node_total
    totals = lax.psum((loss_part, grad_self, grad_neighbor, grad_bias), ("feat", "node"))
    return (logits[None], totals[0], totals[1], totals[2], totals[3])


def solution(mesh):
    return jax.shard_map(
        shards,
        mesh=mesh,
        in_specs=(
            P("node", "feat", None),
            P("node", None, None),
            P("node", None),
            P("node", None, None, None),
            P("node", "feat"),
            P("node", "feat"),
            P(),
            P(),
            P(),
            P(),
            P(),
            P(),
        ),
        out_specs=(P("node", "feat", None), P(), P(), P(), P()),
        check_vma=False,
    )
```

profile of v0, /device:TPU:1, one launch (start us, length us, event | category | flops | bytes accessed | tf_op | source)
XLA Modules:
  0.0 497.7 jit_solution(13302247158256044541)
XLA Ops:
  7.2 0.0 copy-start
  7.2 0.0 all-gather.3.cloned.1.call-start
  7.2 0.7 all-gather.3.cloned.1.call-update
  7.9 0.0 all-gather.5.cloned.1.call-start
  8.0 43.1 %all-gather.3.cloned.1.call-done = bf16[1,128,8192]{2,1,0:T(8,128)(2,1)} async-done(((bf16[1,16,8192]{2,1,0:T(8,128)(2,1)}), bf16[1,128,8192]{2,1,0:T(8,128)(2,1)}) %all-gather.3.cloned.1.call-update) | async-done | bytes 2097168 | tf_op jit(solution)/shard_map/all_gather | solution.py:78
  51.1 3.2 copy.46
  54.3 7.4 %collective-permute-start = (bf16[1,128,8192]{1,2,0:T(8,128)(2,1)S(1)}, bf16[1,128,8192]{1,2,0:T(8,128)(2,1)}, u32[]{:S(2)}, u32[]{:S(2)}) collective-permute-start(bf16[1,128,8192]{1,2,0:T(8,128)(2,1)S(1)} %copy.46), channel_id=1, source_target_pairs={{0,1},{1,2},{2,3},{3,4},{4,5},{5,6},{6,7},{7,8},{8,9},{9,10},{10,1... | collective-permute-start | bytes 6291464 | tf_op jit(solution)/shard_map/ppermute | solution.py:16
  61.7 1.9 collective-permute-start.1
  63.6 0.1 constant_dynamic-slice_fusion
  63.7 0.1 copy.45
  63.8 1.1 constant_dynamic-slice_fusion.2
  64.9 2.8 shift_right_arithmetic.34
  67.7 2.8 copy.44
  70.5 0.1 reshape.85
  70.6 0.1 shift_right_arithmetic.38
  70.7 0.1 fusion.54
  70.7 0.1 fusion.52
  70.8 0.6 multiply_reduce_fusion
  71.4 1.3 fusion.49
  72.7 11.9 %collective-permute-done = bf16[1,128,8192]{1,2,0:T(8,128)(2,1)} collective-permute-done((bf16[1,128,8192]{1,2,0:T(8,128)(2,1)S(1)}, bf16[1,128,8192]{1,2,0:T(8,128)(2,1)}, u32[]{:S(2)}, u32[]{:S(2)}) %collective-permute-start) | collective-permute-done | bytes 2097184 | tf_op jit(solution)/shard_map/ppermute | solution.py:16
  84.6 4.5 collective-permute-done.1
  89.1 5.5 %pad_maximum_fusion.1 = bf16[3,128,8192]{1,2,0:T(8,128)(2,1)} fusion(bf16[1,128,8192]{1,2,0:T(8,128)(2,1)} %collective-permute-done.1, bf16[1,128,8192]{1,2,0:T(8,128)(2,1)S(1)} %copy.46, bf16[1,128,8192]{1,2,0:T(8,128)(2,1)} %collective-permute-done), kind=kLoop, calls=%fused_computation.3 | loop fusion | flops 6291456 | bytes 12582912 | tf_op jit(solution)/shard_map/concatenate | solution.py:18
  94.6 8.6 %copy.49 = bf16[3,64,128,128]{3,2,1,0:T(8,128)(2,1)} copy(bf16[3,64,128,128]{2,3,1,0:T(8,128)(2,1)} %bitcast.67) | data formatting | bytes 12582912 | tf_op jit(solution)/shard_map/transpose | solution.py:46
  103.2 3.7 gather_fusion
  107.0 2.7 fusion.40
  109.8 1.1 fusion.27
  110.8 0.0 all-gather.5.cloned.1.call-update
  110.9 0.0 all-reduce.4.cloned.1.call-start
  110.9 54.4 %all-gather.5.cloned.1.call-done = bf16[8192,256]{1,0:T(8,128)(2,1)} async-done(((bf16[1024,256]{1,0:T(8,128)(2,1)}), bf16[8192,256]{1,0:T(8,128)(2,1)}) %all-gather.5.cloned.1.call-update) | async-done | bytes 4194320 | tf_op jit(solution)/shard_map/all_gather | solution.py:87
  165.3 3.7 collective-permute-start.2
  169.0 1.9 collective-permute-start.3
  170.9 1.4 fusion.59
  172.3 42.4 %collective-permute-done.2 = bf16[1,8192,256]{2,1,0:T(8,128)(2,1)S(1)} collective-permute-done((bf16[1,8192,256]{2,1,0:T(8,128)(2,1)}, bf16[1,8192,256]{2,1,0:T(8,128)(2,1)S(1)}, u32[]{:S(2)}, u32[]{:S(2)}) %collective-permute-start.2) | collective-permute-done | bytes 4194336 | tf_op jit(solution)/shard_map/ppermute | solution.py:16
  214.7 4.3 collective-permute-done.3
  219.0 7.7 %pad_maximum_fusion = bf16[3,8192,256]{2,1,0:T(8,128)(2,1)} fusion(bf16[1,8192,256]{2,1,0:T(8,128)(2,1)S(1)} %collective-permute-done.3, bf16[1,8192,256]{2,1,0:T(8,128)(2,1)} %bitcast.74, bf16[1,8192,256]{2,1,0:T(8,128)(2,1)S(1)} %collective-permute-done.2), kind=kLoop, calls=%fused_computation.2 | loop fusion | flops 12582912 | bytes 25165824 | tf_op jit(solution)/shard_map/concatenate | solution.py:18
  226.8 7.4 %gather_fusion.1 = bf16[64,128,256]{2,1,0:T(8,128)(2,1)} fusion(bf16[192,128,256]{2,1,0:T(8,128)(2,1)} %bitcast.68, s32[1024]{0:T(1024)S(1)} %pad_clamp_fusion), kind=kCustom, calls=%fused_computation.1 | custom fusion | bytes 8388864 | tf_op jit(solution)/shard_map/jit(_take)/gather | solution.py:30
  234.1 3.9 divide_convert_fusion
  238.0 0.4 exponential_reduce_fusion
  238.5 0.3 convert_reduce_fusion
  238.8 0.9 fusion.61
  239.8 0.9 fusion.60
  240.7 0.0 all-reduce.4.cloned.1.call-update
  240.7 0.6 multiply_reduce_fusion.1
  242.0 77.7 %all-reduce = (f32[]{:T(128)}, f32[172]{0:T(256)}) all-reduce(f32[]{:T(128)S(6)} %div.31, f32[172]{0:T(256)S(1)} %get-tuple-element.36), channel_id=1, replica_groups=mesh['feat'=8,'node'=32] {'feat','node'}, use_global_device_ids=true, to_apply=%region_4.5 | all-reduce | flops 173 | bytes 1384 | tf_op jit(solution)/shard_map/psum | solution.py:112
  319.7 1.6 copy.52
  321.3 166.7 %all-reduce.4.cloned.1.call-done = (f32[256,172]{0,1:T(8,128)}, f32[256,172]{0,1:T(8,128)}) async-done(((f32[256,172]{0,1:T(8,128)}, f32[256,172]{0,1:T(8,128)}), (f32[256,172]{0,1:T(8,128)}, f32[256,172]{0,1:T(8,128)})) %all-reduce.4.cloned.1.call-update) | async-done | bytes 352272 | tf_op jit(solution)/shard_map/psum | solution.py:112
  487.9 1.6 copy.59
  489.5 1.6 copy.60
  (31 shorter events, 0.1 us)
Async XLA Ops:
  7.2 230.9 %copy-start = (bf16[256,172]{0,1:T(8,128)(2,1)S(1)}, bf16[256,172]{0,1:T(8,128)(2,1)}, u32[]{:S(2)}) copy-start(bf16[256,172]{0,1:T(8,128)(2,1)} %param.22) | copy-start | bytes 264196
  7.2 56.4 %copy-start.8 = (s32[1,64,8]{1,2,0:T(8,128)S(1)}, s32[1,64,8]{1,2,0:T(8,128)}, u32[]{:S(2)}) copy-start(s32[1,64,8]{1,2,0:T(8,128)} %param.13) | copy-start | bytes 6148
  7.2 43.9 %all-gather.3.cloned.1.call-start = ((), (), s32[]{:S(2)}) async-start(), calls=%async_computation | async-start | bytes 2359296 | tf_op jit(solution)/shard_map/all_gather | solution.py:78
  7.9 157.4 %all-gather.5.cloned.1.call-start = ((), (), s32[]{:S(2)}) async-start(), calls=%async_computation.1 | async-start | bytes 4718592 | tf_op jit(solution)/shard_map/all_gather | solution.py:87
  54.3 30.4 %collective-permute-start = (bf16[1,128,8192]{1,2,0:T(8,128)(2,1)S(1)}, bf16[1,128,8192]{1,2,0:T(8,128)(2,1)}, u32[]{:S(2)}, u32[]{:S(2)}) collective-permute-start(bf16[1,128,8192]{1,2,0:T(8,128)(2,1)S(1)} %copy.46), channel_id=1, source_target_pairs={{0,1},{1,2},{2,3},{3,4},{4,5},{5,6},{6,7},{7,8},{8,9},{9,10},{10,1... | collective-permute-start | bytes 6291464 | tf_op jit(solution)/shard_map/ppermute | solution.py:16
  61.7 27.5 %collective-permute-start.1 = (bf16[1,128,8192]{1,2,0:T(8,128)(2,1)S(1)}, bf16[1,128,8192]{1,2,0:T(8,128)(2,1)}, u32[]{:S(2)}, u32[]{:S(2)}) collective-permute-start(bf16[1,128,8192]{1,2,0:T(8,128)(2,1)S(1)} %copy.46), channel_id=1, source_target_pairs={{1,0},{2,1},{3,2},{4,3},{5,4},{6,5},{7,6},{8,7},{9,8},{10,9},{11,1... | collective-permute-start | bytes 6291464 | tf_op jit(solution)/shard_map/ppermute | solution.py:17
  64.9 5.8 %copy-start.12 = (s32[1,64]{1,0:T(1,128)S(1)}, s32[1,64]{1,0:T(1,128)}, u32[]{:S(2)}) copy-start(s32[1,64]{1,0:T(1,128)} %param.14) | copy-start | bytes 772
  64.9 6.6 %copy-start.5 = (bf16[128,256]{1,0:T(8,128)(2,1)S(1)}, bf16[128,256]{1,0:T(8,128)(2,1)}, u32[]{:S(2)}) copy-start(bf16[128,256]{1,0:T(8,128)(2,1)} %param.18) | copy-start | bytes 196612
  70.5 1.0 copy-start.2
  107.0 2.7 copy-start.6
  107.0 2.7 copy-start.10
  107.0 63.9 %copy-start.9 = (s32[1,1024]{1,0:T(1,128)S(1)}, s32[1,1024]{1,0:T(1,128)}, u32[]{:S(2)}) copy-start(s32[1,1024]{1,0:T(1,128)} %param.17) | copy-start | bytes 12292
  107.0 63.9 %copy-start.4 = (bf16[256,172]{0,1:T(8,128)(2,1)S(1)}, bf16[256,172]{0,1:T(8,128)(2,1)}, u32[]{:S(2)}) copy-start(bf16[256,172]{0,1:T(8,128)(2,1)} %param.21) | copy-start | bytes 264196
  110.9 377.1 %all-reduce.4.cloned.1.call-start = ((), (), s32[]{:S(2)}) async-start(), calls=%async_computation.2 | async-start | bytes 720896 | tf_op jit(solution)/shard_map/psum | solution.py:112
  165.3 49.4 %collective-permute-start.2 = (bf16[1,8192,256]{2,1,0:T(8,128)(2,1)}, bf16[1,8192,256]{2,1,0:T(8,128)(2,1)S(1)}, u32[]{:S(2)}, u32[]{:S(2)}) collective-permute-start(bf16[1,8192,256]{2,1,0:T(8,128)(2,1)} %bitcast.72), channel_id=1, source_target_pairs={{0,1},{1,2},{2,3},{3,4},{4,5},{5,6},{6,7},{7,8},{8,9},{9,10},{10,1... | collective-permute-start | bytes 12582920 | tf_op jit(solution)/shard_map/ppermute | solution.py:16
  169.0 50.0 %collective-permute-start.3 = (bf16[1,8192,256]{2,1,0:T(8,128)(2,1)}, bf16[1,8192,256]{2,1,0:T(8,128)(2,1)S(1)}, u32[]{:S(2)}, u32[]{:S(2)}) collective-permute-start(bf16[1,8192,256]{2,1,0:T(8,128)(2,1)} %bitcast.73), channel_id=1, source_target_pairs={{1,0},{2,1},{3,2},{4,3},{5,4},{6,5},{7,6},{8,7},{9,8},{10,9},{11,1... | collective-permute-start | bytes 12582920 | tf_op jit(solution)/shard_map/ppermute | solution.py:17
  226.8 7.4 %copy-start.3 = (s32[8,8,128,16]{2,3,1,0:T(8,128)S(1)}, s32[8,8,128,16]{2,3,1,0:T(8,128)}, u32[]{:S(2)}) copy-start(s32[8,8,128,16]{2,3,1,0:T(8,128)} %copy-done.2) | copy-start | bytes 1572868
  234.1 3.9 copy-start.7
  234.1 3.9 copy-start.11
  238.0 1.7 copy-start.1
Sparse Core Ops, SparseCore 0:
  9.8 41.1 all-gather.2
  111.0 54.2 all-gather.4
  240.8 247.0 all-reduce.3
where the time goes:
time: 499 us; the launch traced here: 498 us
  waiting for transfers between devices  328 us (66%)
  blocking collectives  77.7 us (16%)
  local copies, waits for them, and re-layouts  34.8 us (7%)
  starting transfers between devices  15 us (3%)
  other arithmetic  14.9 us (3%)
  between operations  14.7 us (3%)
  matrix products  12.6 us (3%)
    psum x1, waiting for transfers between devices, shards(): lax.psum((loss_part, grad_self, grad_neighbor, grad_bias), ('feat', 'node'))  167 us
    psum x1, blocking collectives, shards(): lax.psum((loss_part, grad_self, grad_neighbor, grad_bias), ('feat', 'node'))  77.7 us
    all_gather x1, waiting for transfers between devices, shards(): block_hidden = lax.all_gather(hidden, 'feat', axis=0, tiled=True)  54.4 us
    ppermute x2, waiting for transfers between devices, with_halo(): before = lax.ppermute(last, axis, up)  54.3 us
    all_gather x1, waiting for transfers between devices, shards(): full_width = lax.all_gather(features, 'feat', axis=1, tiled=True)  43.1 us
    concatenate x2, other arithmetic, with_halo(): value = jnp.concatenate([before, value, after], axis=dim)  13.2 us
    gather x2, local copies, waits for them, and re-layouts, aggregate(): picked = jnp.take(table, columns, axis=0)  11.1 us
    ppermute x2, starting transfers between devices, with_halo(): before = lax.ppermute(last, axis, up)  11 us
  transfers between devices with their start and end apart: 7, of which 7 were waited for; matrix products, arithmetic and copies ran while one was open for 3% of the time, Pallas kernels for 0%

commit v1 on v0

v1 whole, which is shorter than its diff:
```python
import functools
import math

import jax
import jax.numpy as jnp
from jax import lax
from jax.experimental import pallas as pl
from jax.experimental.pallas import tpu as pltpu
from jax.sharding import PartitionSpec as P

MESH = pl.DeviceIdType.MESH
F32 = jnp.float32
BF16 = jnp.bfloat16
NT_DIMS = (((1,), (1,)), ((), ()))
LANES = 128
SLOTS = 8
BLOCK = 8192
TILES = 64
GROUPS = 8
GROUP = 1024
CLS = 172
CLS_PAD = 176
PIECE = 24
HALF = 384


def iota(shape, axis):
    return lax.broadcasted_iota(jnp.int32, shape, axis)


def lanes(index, width=LANES):
    return pl.ds(pl.multiple_of(index * width, width), width)


def rows(index, height):
    return pl.ds(pl.multiple_of(index * height, height), height)


def loop(low, high, body):
    def step(i, carry):
        body(i)
        return carry

    lax.fori_loop(low, high, step, 0)


def permutation():
    j, p = iota((LANES, LANES), 0), iota((LANES, LANES), 1)
    return (j == 8 * (p % 16) + p // 16).astype(F32).astype(BF16)


def exchange_bits(words):
    group = iota(words.shape, 1) // 16
    for level, low_bits in ((0, 0x55555555), (1, 0x33333333), (2, 0x0F0F0F0F)):
        distance = 1 << level
        upper = ((group >> level) & 1) == 1
        keep = jnp.where(upper, ~jnp.int32(low_bits), jnp.int32(low_bits))
        from_above = pltpu.roll(words, LANES - 16 * distance, 1) << distance
        from_below = pltpu.roll(words, 16 * distance, 1) >> distance
        words = (words & keep) | (jnp.where(upper, from_below, from_above) & ~keep)
    return words


def unpack_row_tile(t, count_ref, bits, adj):
    limit = jnp.full((8, LANES), count_ref[0, t], jnp.int32)
    for pair in range(SLOTS // 2):
        packed = None
        for part in range(4):
            slot, half = 2 * pair + part // 2, part % 2
            piece = bits[t, pl.ds(64 * half + slot, 8, stride=8), :]
            piece = jnp.where(limit > slot, piece, 0) << (8 * part)
            packed = piece if packed is None else packed | piece
        packed = exchange_bits(packed)
        for side in range(2):
            slot = 2 * pair + side
            for low in range(8):
                first = (packed >> (16 * side + low)) & 1
                second = (packed >> (16 * side + 8 + low)) & 1
                both = jnp.concatenate([first, second], axis=0).astype(F32).astype(BF16)
                adj[t, 16 * low : 16 * low + 16, LANES * slot : LANES * (slot + 1)] = both


def picked_tiles(t, first_column, column_ref, table):
    parts = []
    for slot in range(SLOTS):
        index = jnp.clip(column_ref[t, slot] - first_column, 0, 3 * TILES - 1)
        parts.append(table[index])
    return jnp.concatenate(parts, axis=1)


def kernel(
    scale,
    features,
    column_ref,
    count_ref,
    bit_words,
    labels,
    train_mask,
    first_self,
    first_neighbor,
    first_bias,
    second_self,
    second_neighbor,
    second_bias,
    logits_out,
    total_out,
    feats,
    bits,
    adj,
    table1,
    stage1,
    inputs1,
    table2,
    stage2,
    parts1,
    parts2,
    hidden,
    mean2,
    inv_degree,
    w1,
    w2,
    b1,
    b2,
    class_mask,
    logits,
    logits_rows,
    turn_left,
    turn_right,
    grad,
    payload,
    core_in,
    half_sum,
    plane_in,
    line_in,
    total,
    bit_sem,
    local_sem,
    halo1_send,
    halo1_recv,
    x_send,
    x_recv,
    m_send,
    m_recv,
    h_send,
    h_recv,
    halo2_send,
    halo2_recv,
    n_send,
    n_recv,
    core_send,
    core_recv,
    plane_send,
    plane_recv,
    line_send,
    line_recv,
    back_send,
    back_recv,
):
    z = lax.axis_index("feat")
    node = lax.axis_index("node")
    core = lax.rem(node, 2)
    plane = lax.div(node, 2)
    up = lax.rem(node + 1, 32)
    down = lax.rem(node + 31, 32)
    core_peer = plane * 2 + 1 - core
    first_column = (node - 1) * TILES

    def around(offset):
        return lax.rem(z + offset, GROUPS)

    def plane_peer(offset):
        return lax.rem(plane + offset, 16)

    def send(src, dst, send_sem, recv_sem, device):
        return pltpu.make_async_remote_copy(
            src_ref=src,
            dst_ref=dst,
            send_sem=send_sem,
            recv_sem=recv_sem,
            device_id=device,
            device_id_type=MESH,
        )

    barrier = pltpu.get_barrier_semaphore()

    def greet(device):
        pl.semaphore_signal(barrier, inc=1, device_id=device, device_id_type=MESH)

    loop(1, GROUPS, lambda o: greet((around(o), node)))
    loop(1, 16, lambda o: greet((z, plane_peer(o) * 2 + core)))
    greet((z, up))
    greet((z, down))

    feature_copy = pltpu.make_async_copy(features.at[0], feats, local_sem.at[0])
    feature_copy.start()

    def bit_copy(r):
        return pltpu.make_async_copy(
            bit_words.at[0, :, :, lanes(r)], bits.at[:, rows(r, 8), :], bit_sem.at[r]
        )

    loop(0, 16, lambda r: bit_copy(r).start())

    perm = permutation()
    feature_copy.wait()

    def permute_features(t):
        moved = jnp.dot(feats[:, lanes(t)], perm, preferred_element_type=F32)
        table1[TILES + t] = moved.astype(BF16)

    loop(0, TILES, permute_features)
    pl.semaphore_wait(barrier, 24)

    own1 = table1.at[pl.ds(TILES, TILES)]
    to_up1 = send(own1, table1.at[pl.ds(0, TILES)], halo1_send.at[0], halo1_recv.at[0], (z, up))
    to_down1 = send(own1, table1.at[pl.ds(2 * TILES, TILES)], halo1_send.at[1], halo1_recv.at[1], (z, down))
    to_up1.start()
    to_down1.start()

    def send_x(group, source):
        return send(
            table1.at[pl.ds(TILES + 8 * group, 8)],
            inputs1.at[source],
            x_send.at[group],
            x_recv.at[source],
            (group, node),
        )

    def send_m(group, source):
        return send(
            stage1.at[pl.ds(8 * group, 8)],
            inputs1.at[8 + source],
            m_send.at[group],
            m_recv.at[source],
            (group, node),
        )

    def send_h(group, source):
        return send(
            parts1.at[group],
            table2.at[pl.ds(TILES + 8 * source, 8)],
            h_send.at[group],
            h_recv.at[source],
            (group, node),
        )

    def send_n(group, source):
        return send(
            stage2.at[pl.ds(8 * group, 8)],
            parts2.at[source],
            n_send.at[group],
            n_recv.at[source],
            (group, node),
        )

    loop(1, GROUPS, lambda o: send_x(around(o), z).start())
    x_own = pltpu.make_async_copy(
        table1.at[pl.ds(TILES + 8 * z, 8)], inputs1.at[z], local_sem.at[1]
    )
    x_own.start()

    eye = (iota((256, 256), 0) == iota((256, 256), 1)).astype(F32).astype(BF16)
    for part, weight in enumerate((first_self, first_neighbor)):
        turned = lax.dot_general(eye, weight[...], NT_DIMS, preferred_element_type=F32)
        w1[:, LANES * part : LANES * (part + 1)] = turned.astype(BF16)
    pick = (iota((CLS_PAD, CLS), 0) == iota((CLS_PAD, CLS), 1)).astype(F32)
    for part, weight in enumerate((second_self, second_neighbor)):
        turned = lax.dot_general(pick.astype(BF16), weight[...], NT_DIMS, preferred_element_type=F32)
        w2[:, 256 * part : 256 * (part + 1)] = turned.astype(BF16)
    column1 = jnp.sum(
        jnp.where(iota((256, 256), 0) == iota((256, 256), 1), first_bias[...], 0.0),
        axis=1,
        keepdims=True,
    )
    b1[...] = jnp.broadcast_to(column1, (256, LANES))
    column2 = jnp.sum(jnp.where(pick > 0.5, second_bias[...], 0.0), axis=1, keepdims=True)
    column2 = jnp.where(iota((CLS_PAD, 1), 0) < CLS, column2, -1e30)
    b2[...] = jnp.broadcast_to(column2, (CLS_PAD, LANES))
    both = jnp.where(
        iota((16, GROUP), 0) < 8,
        jnp.broadcast_to(labels[...].astype(F32), (16, GROUP)),
        jnp.broadcast_to(train_mask[...].astype(F32), (16, GROUP)),
    ).astype(BF16)
    for u in range(8):
        span = slice(LANES * u, LANES * (u + 1))
        class_mask[:, span] = jnp.dot(both[:, span], perm, preferred_element_type=F32)

    loop(0, 16, lambda r: bit_copy(r).wait())
    loop(0, TILES, lambda t: unpack_row_tile(t, count_ref, bits, adj))

    to_up1.wait_recv()
    to_down1.wait_recv()

    def first_tile(t):
        values = picked_tiles(t, first_column, column_ref, table1)
        stacked = jnp.concatenate([values, jnp.ones((16, SLOTS * LANES), BF16)], axis=0)
        sums = lax.dot_general(stacked, adj[t], NT_DIMS, preferred_element_type=F32)
        inverse = 1.0 / jnp.maximum(sums[16:24], 1.0)
        inv_degree[t] = inverse
        stage1[t] = (sums[:16] * inverse[:1]).astype(BF16)

    def first_group(o):
        group = around(o)
        loop(0, 8, lambda u: first_tile(group * 8 + u))

        @pl.when(o < GROUPS)
        def _():
            send_m(group, z).start()

    loop(1, GROUPS + 1, first_group)
    m_own = pltpu.make_async_copy(
        stage1.at[pl.ds(8 * z, 8)], inputs1.at[8 + z], local_sem.at[2]
    )
    m_own.start()
    x_own.wait()
    m_own.wait()
    loop(1, GROUPS, lambda o: send_x(z, around(o)).wait_recv())
    loop(1, GROUPS, lambda o: send_m(z, around(o)).wait_recv())

    def first_dense(u):
        node_inputs = inputs1[:, u].reshape(256, LANES)
        total1 = jnp.dot(w1[...], node_inputs, preferred_element_type=F32)
        activated = jnp.maximum(total1 + b1[...], 0.0).astype(BF16)
        hidden[:, lanes(u)] = activated
        parts1[:, u] = activated.reshape(GROUPS, 32, LANES)

    loop(0, 8, first_dense)
    loop(1, GROUPS, lambda o: send_h(around(o), z).start())
    table2[pl.ds(TILES + 8 * z, 8)] = parts1[z]

    def halo2(group, side, device):
        return send(
            table2.at[pl.ds(TILES + 8 * group, 8)],
            table2.at[pl.ds(2 * TILES * side + 8 * group, 8)],
            halo2_send.at[side, group],
            halo2_recv.at[side, group],
            (z, device),
        )

    def forward(group):
        halo2(group, 0, up).start()
        halo2(group, 1, down).start()

    forward(z)

    def pass_on(o):
        group = around(o)
        send_h(z, group).wait_recv()
        forward(group)

    loop(1, GROUPS, pass_on)

    def halo2_arrived(group):
        halo2(group, 0, up).wait_recv()
        halo2(group, 1, down).wait_recv()

    loop(0, GROUPS, halo2_arrived)

    def second_tile(t):
        values = picked_tiles(t, first_column, column_ref, table2)
        sums = lax.dot_general(values, adj[t], NT_DIMS, preferred_element_type=F32)
        stage2[t] = (sums * inv_degree[t][:1]).astype(BF16)

    def second_group(o):
        group = around(o)
        loop(0, 8, lambda u: second_tile(group * 8 + u))

        @pl.when(o < GROUPS)
        def _():
            send_n(group, z).start()

    loop(1, GROUPS + 1, second_group)
    parts2[z] = stage2[pl.ds(8 * z, 8)]
    loop(1, GROUPS, lambda o: send_n(z, around(o)).wait_recv())

    def second_dense(u, loss):
        span = lanes(u)
        mean2[:, span] = parts2[:, u].reshape(256, LANES)
        score = (
            jnp.dot(w2[:, :256], hidden[:, span], preferred_element_type=F32)
            + jnp.dot(w2[:, 256:], mean2[:, span], preferred_element_type=F32)
            + b2[...]
        )
        logits[:, span] = score
        exponent = jnp.exp(score)
        class_total = jnp.sum(exponent, axis=0, keepdims=True)
        label = class_mask[0:1, span].astype(jnp.int32)
        weight = class_mask[8:9, span]
        chosen = iota((CLS_PAD, LANES), 0) == label
        own_score = jnp.sum(jnp.where(chosen, score, 0.0), axis=0, keepdims=True)
        slope = exponent * (1.0 / class_total) - jnp.where(chosen, 1.0, 0.0)
        grad[0:CLS_PAD, span] = (slope * (weight * scale)).astype(BF16)
        return loss + (jnp.log(class_total) - own_score) * weight

    grad[CLS_PAD:256, :] = jnp.zeros((256 - CLS_PAD, GROUP), BF16)
    loss_lanes = lax.fori_loop(0, 8, second_dense, jnp.zeros((1, LANES), F32))
    loss = jnp.sum(loss_lanes, axis=1, keepdims=True) * (scale * scale)
    bias = jnp.sum(grad[...].astype(F32), axis=1, keepdims=True)
    payload[0:256] = lax.dot_general(hidden[...], grad[0:128], NT_DIMS, preferred_element_type=F32)
    payload[256:512] = lax.dot_general(mean2[...], grad[0:128], NT_DIMS, preferred_element_type=F32)
    tail = grad[128:256]
    tail_self = lax.dot_general(hidden[...], tail, NT_DIMS, preferred_element_type=F32)
    tail_neighbor = lax.dot_general(mean2[...], tail, NT_DIMS, preferred_element_type=F32)
    last = iota((256, LANES), 1) == 127
    extra = jnp.where(iota((256, LANES), 0) == 200, loss, bias)
    payload[512:768] = jnp.where(last, extra, tail_self + pltpu.roll(tail_neighbor, 64, 1))

    core_copy = send(
        payload.at[rows(1 - core, HALF), :], core_in, core_send.at[0], core_recv.at[0], (z, core_peer)
    )
    core_copy.start()

    def turn(u):
        turned = logits[:, lanes(u)].T
        for low in range(8):
            place = pl.ds(low, 16, stride=8)
            turn_left[place, :] = turned[16 * low : 16 * low + 16, :LANES]
            turn_right[place, : CLS_PAD - LANES] = turned[16 * low : 16 * low + 16, LANES:]
        logits_rows[rows(u, LANES), :LANES] = turn_left[...]
        logits_rows[rows(u, LANES), LANES:] = turn_right[:, : CLS - LANES]

    loop(0, 8, turn)
    logits_copy = pltpu.make_async_copy(logits_rows, logits_out.at[0], local_sem.at[3])
    logits_copy.start()

    core_copy.wait_recv()
    half_sum[...] = payload[rows(core, HALF), :] + core_in[...]

    def plane_copy(target, source):
        return send(
            half_sum.at[rows(target, PIECE), :],
            plane_in.at[source],
            plane_send.at[target],
            plane_recv.at[source],
            (z, target * 2 + core),
        )

    loop(1, 16, lambda o: plane_copy(plane_peer(o), plane).start())
    plane_in[plane] = half_sum[rows(plane, PIECE), :]
    loop(1, 16, lambda o: plane_copy(plane, plane_peer(o)).wait_recv())
    line_in[z] = jnp.sum(plane_in[...], axis=0)

    def line_copy(target, source):
        return send(
            line_in.at[source], line_in.at[source], line_send.at[target], line_recv.at[source], (target, node)
        )

    loop(1, GROUPS, lambda o: line_copy(around(o), z).start())
    loop(1, GROUPS, lambda o: line_copy(z, around(o)).wait_recv())
    total[rows(core * 16 + plane, PIECE), :] = jnp.sum(line_in[...], axis=0)

    def back_copy(target, source):
        part = total.at[rows(core * 16 + source, PIECE), :]
        return send(part, part, back_send.at[target], back_recv.at[source], (z, target * 2 + core))

    loop(1, 16, lambda o: back_copy(plane_peer(o), plane).start())
    loop(1, 16, lambda o: back_copy(plane, plane_peer(o)).wait_recv())

    def half_copy(which):
        part = total.at[rows(which, HALF), :]
        return send(part, part, core_send.at[1], core_recv.at[1], (z, core_peer))

    half_copy(core).start()
    half_copy(1 - core).wait_recv()
    result = pltpu.make_async_copy(total, total_out, local_sem.at[4])
    result.start()

    to_up1.wait_send()
    to_down1.wait_send()

    def left_line(o):
        group = around(o)
        send_x(group, z).wait_send()
        send_m(group, z).wait_send()
        send_h(group, z).wait_send()
        send_n(group, z).wait_send()
        line_copy(group, z).wait_send()

    loop(1, GROUPS, left_line)

    def left_halo(group):
        halo2(group, 0, up).wait_send()
        halo2(group, 1, down).wait_send()

    loop(0, GROUPS, left_halo)

    def left_plane(o):
        target = plane_peer(o)
        plane_copy(target, plane).wait_send()
        back_copy(target, plane).wait_send()

    loop(1, 16, left_plane)
    core_copy.wait_send()
    half_copy(core).wait_send()
    logits_copy.wait()
    result.wait()


def shards(
    features,
    tile_columns,
    tile_count,
    tile_bits,
    labels,
    train_mask,
    first_self,
    first_neighbor,
    first_bias,
    second_self,
    second_neighbor,
    second_bias,
):
    node_total = features.shape[2] * lax.axis_size("node")
    dma = pltpu.SemaphoreType.DMA
    vmem = pl.BlockSpec(memory_space=pltpu.VMEM)
    smem = pl.BlockSpec(memory_space=pltpu.SMEM)
    anywhere = pl.BlockSpec(memory_space=pl.ANY)
    logits, total = pl.pallas_call(
        functools.partial(kernel, 1.0 / math.sqrt(node_total)),
        out_shape=(
            jax.ShapeDtypeStruct((1, GROUP, CLS), F32),
            jax.ShapeDtypeStruct((2 * HALF, LANES), F32),
        ),
        in_specs=[anywhere, smem, smem, anywhere] + [vmem] * 8,
        out_specs=(anywhere, anywhere),
        scratch_shapes=[
            pltpu.VMEM((16, BLOCK), BF16),
            pltpu.VMEM((TILES, 128, LANES), jnp.int32),
            pltpu.VMEM((TILES, LANES, SLOTS * LANES), BF16),
            pltpu.VMEM((3 * TILES, 16, LANES), BF16),
            pltpu.VMEM((TILES, 16, LANES), BF16),
            pltpu.VMEM((2 * GROUPS, 8, 16, LANES), BF16),
            pltpu.VMEM((3 * TILES, 32, LANES), BF16),
            pltpu.VMEM((TILES, 32, LANES), BF16),
            pltpu.VMEM((GROUPS, 8, 32, LANES), BF16),
            pltpu.VMEM((GROUPS, 8, 32, LANES), BF16),
            pltpu.VMEM((256, GROUP), BF16),
            pltpu.VMEM((256, GROUP), BF16),
            pltpu.VMEM((TILES, 8, LANES), F32),
            pltpu.VMEM((256, 256), BF16),
            pltpu.VMEM((CLS_PAD, 512), BF16),
            pltpu.VMEM((256, LANES), F32),
            pltpu.VMEM((CLS_PAD, LANES), F32),
            pltpu.VMEM((16, GROUP), F32),
            pltpu.VMEM((CLS_PAD, GROUP), F32),
            pltpu.VMEM((GROUP, CLS), F32),
            pltpu.VMEM((LANES, LANES), F32),
            pltpu.VMEM((LANES, LANES), F32),
            pltpu.VMEM((256, GROUP), BF16),
            pltpu.VMEM((2 * HALF, LANES), F32),
            pltpu.VMEM((HALF, LANES), F32),
            pltpu.VMEM((HALF, LANES), F32),
            pltpu.VMEM((16, PIECE, LANES), F32),
            pltpu.VMEM((GROUPS, PIECE, LANES), F32),
            pltpu.VMEM((2 * HALF, LANES), F32),
            dma((16,)),
            dma((5,)),
            dma((2,)),
            dma((2,)),
            dma((GROUPS,)),
            dma((GROUPS,)),
            dma((GROUPS,)),
            dma((GROUPS,)),
            dma((GROUPS,)),
            dma((GROUPS,)),
            dma((2, GROUPS)),
            dma((2, GROUPS)),
            dma((GROUPS,)),
            dma((GROUPS,)),
            dma((2,)),
            dma((2,)),
            dma((16,)),
            dma((16,)),
            dma((GROUPS,)),
            dma((GROUPS,)),
            dma((16,)),
            dma((16,)),
        ],
        compiler_params=pltpu.CompilerParams(
            collective_id=0, has_side_effects=True, vmem_limit_bytes=52 * 1024 * 1024
        ),
    )(
        features,
        tile_columns[0],
        tile_count,
        tile_bits,
        labels,
        train_mask,
        first_self,
        first_neighbor,
        first_bias[None],
        second_self,
        second_neighbor,
        second_bias[None],
    )
    tail = total[512:]
    grad_self = jnp.concatenate([total[:256], tail[:, : CLS - 128]], axis=1)
    grad_neighbor = jnp.concatenate([total[256:512], tail[:, 64 : CLS - 64]], axis=1)
    return (logits, tail[200, 127], grad_self, grad_neighbor, tail[:CLS, 127])


def solution(mesh):
    return jax.shard_map(
        shards,
        mesh=mesh,
        in_specs=(
            P("node", "feat", None),
            P("node", None, None),
            P("node", None),
            P("node", None, None, None),
            P("node", "feat"),
            P("node", "feat"),
            P(),
            P(),
            P(),
            P(),
            P(),
            P(),
        ),
        out_specs=(P("node", "feat", None), P(), P(), P(), P()),
        check_vma=False,
    )
```

time: 499 us -> 133 us (0.27)
  waiting for transfers between devices: 328 us -> 0 us
  Pallas kernels: 0 us -> 117 us
  blocking collectives: 77.7 us -> 0 us
  local copies, waits for them, and re-layouts: 34.8 us -> 14.8 us
  starting transfers between devices: 15 us -> 0 us
  other arithmetic: 14.9 us -> 0.04 us
  between operations: 14.7 us -> 0.69 us
  matrix products: 12.6 us -> 0 us
    psum x1 -> x0, waiting for transfers between devices: 167 us -> none  [shards(): lax.psum((loss_part, grad_self, grad_neighbor, grad_bias), ('feat', 'node'))]
    pallas_call x0 -> x1, Pallas kernels: none -> 117 us  [shards(): pl.pallas_call(functools.partial(kernel, 1.0 / math.sqrt(node_total)), ou...]
    all_gather x2 -> x0, waiting for transfers between devices: 97.5 us -> none  [the longest x1 54.4 us: shards(): block_hidden = lax.all_gather(hidden, 'feat', axis=0, tiled=True)]
    psum x1 -> x0, blocking collectives: 77.7 us -> none  [shards(): lax.psum((loss_part, grad_self, grad_neighbor, grad_bias), ('feat', 'node'))]
    ppermute x4 -> x0, waiting for transfers between devices: 63.1 us -> none  [the longest x2 54.3 us: with_halo(): before = lax.ppermute(last, axis, up)]
    ppermute x4 -> x0, starting transfers between devices: 14.9 us -> none  [the longest x2 11 us: with_halo(): before = lax.ppermute(last, axis, up)]
    concatenate x2 -> x1, other arithmetic: 13.2 us -> 0.04 us  [shards(): grad_self = jnp.concatenate([total[:256], tail[:, :CLS - 128]], axis=1)]
    dot_general x8 -> x0, matrix products: 12.6 us -> none  [the longest x2 6.55 us: aggregate(): jnp.einsum(pattern, bit_table.astype(jnp.bfloat16), picked, preferred_ele...]
  transfers between devices with their start and end apart: 7 -> 0, of which waited for: 7 -> 0; matrix products, arithmetic and copies ran while one was open for 3% -> 0% of each run, Pallas kernels for 0% -> 0%
where the time goes in v1:
time: 133 us
  Pallas kernels  117 us (88%)
  local copies, waits for them, and re-layouts  14.8 us (11%)
    pallas_call x1, Pallas kernels, shards(): pl.pallas_call(functools.partial(kernel, 1.0 / math.sqrt(node_total)), ou...  117 us
    unnamed x22, local copies, waits for them, and re-layouts  13.4 us

profile of v1, /device:TPU:1, one launch (start us, length us, event | category | flops | bytes accessed | tf_op | source)
XLA Modules:
  0.0 132.7 jit_solution(16909582738466687447)
XLA Ops:
  0.6 0.8 copy.23
  1.4 1.0 copy.24.second_self
  2.4 1.0 copy.25.second_neighbor
  3.4 0.0 copy-start
  3.4 0.9 copy-done
  4.3 0.0 copy-start.1
  4.3 0.8 copy-done.1
  5.2 0.0 copy-start.2
  5.2 0.8 copy-done.2
  6.0 0.0 copy-start.3
  6.0 0.7 copy-done.3
  6.7 0.0 copy-start.4
  6.7 0.7 copy-done.4
  7.4 0.0 copy-start.5
  7.4 0.7 copy-done.5
  8.1 0.0 copy-start.6
  8.1 0.7 copy-done.6
  8.8 0.0 copy-start.7
  8.8 0.7 copy-done.7
  9.4 117.2 %shard_map.155 = (f32[1,1024,172]{2,1,0:T(8,128)}, f32[768,128]{1,0:T(8,128)S(1)}) custom-call(bf16[1,16,8192]{2,1,0:T(8,128)(2,1)S(1)} %copy-done, s32[64,8]{1,0:T(8,128)S(1)} %bitcast.4, s32[1,64]{1,0:T(1,128)S(1)} %copy-done.7, s32[1,64,8,2048]{3,2,1,0:T(8,128)} %bit_words.1, s32[1,1024]{1,0:T(1,128)S(1)} %copy-done.3, s32[1,1024]{1,0:T(1,128)S(1)} %copy-done.4, ...), custom_call_target="tpu_custom_call" | custom-call | tf_op jit(solution)/shard_map/pallas_call | solution.py:518
  126.6 0.6 slice.23
  127.2 3.1 %copy.26 = f32[1,1024,172]{1,0,2:T(1,128)} copy(f32[1,1024,172]{2,1,0:T(8,128)} %get-tuple-element.14) | data formatting | bytes 1409024
  130.3 0.7 slice_reduce_fusion
  131.0 0.1 fusion.1
  131.2 0.8 copy.27
  132.0 0.8 copy.28
  (2 shorter events, 0.1 us)
Async XLA Ops:
  3.4 1.0 copy-start
  4.3 0.8 copy-start.1
  5.2 0.8 copy-start.2
  6.0 0.7 copy-start.3
  6.7 0.7 copy-start.4
  7.4 0.7 copy-start.5
  8.1 0.7 copy-start.6
  8.8 0.7 copy-start.7

commit v2 on v1

--- a/solution.py
+++ b/solution.py
@@ -83,7 +83,7 @@
 def picked_tiles(t, first_column, column_ref, table):
     parts = []
     for slot in range(SLOTS):
-        index = jnp.clip(column_ref[t, slot] - first_column, 0, 3 * TILES - 1)
+        index = jnp.clip(column_ref[slot, t] - first_column, 0, 3 * TILES - 1)
         parts.append(table[index])
     return jnp.concatenate(parts, axis=1)
 
@@ -91,9 +91,24 @@
 def kernel(
     scale,
     features,
+    bit_words,
+    columns_in,
+    count_in,
+    labels_in,
+    train_mask_in,
+    first_self_in,
+    first_neighbor_in,
+    first_bias_in,
+    second_self_in,
+    second_neighbor_in,
+    second_bias_in,
+    logits_out,
+    grad_self_out,
+    grad_neighbor_out,
+    grad_bias_out,
+    loss_out,
     column_ref,
     count_ref,
-    bit_words,
     labels,
     train_mask,
     first_self,
@@ -102,8 +117,10 @@
     second_self,
     second_neighbor,
     second_bias,
-    logits_out,
-    total_out,
+    grad_self,
+    grad_neighbor,
+    grad_bias,
+    loss_held,
     feats,
     bits,
     adj,
@@ -117,15 +134,12 @@
     hidden,
     mean2,
     inv_degree,
+    hidden_true,
     w1,
     w2,
     b1,
     b2,
-    class_mask,
-    logits,
     logits_rows,
-    turn_left,
-    turn_right,
     grad,
     payload,
     core_in,
@@ -134,6 +148,7 @@
     line_in,
     total,
     bit_sem,
+    small_sem,
     local_sem,
     halo1_send,
     halo1_recv,
@@ -181,6 +196,7 @@
             device_id_type=MESH,
         )
 
+    closing = []
     barrier = pltpu.get_barrier_semaphore()
 
     def greet(device):
@@ -200,6 +216,25 @@
         )
 
     loop(0, 16, lambda r: bit_copy(r).start())
+    small = [
+        pltpu.make_async_copy(src, dst, small_sem.at[i])
+        for i, (src, dst) in enumerate(
+            (
+                (columns_in, column_ref),
+                (count_in, count_ref),
+                (first_self_in, first_self),
+                (first_neighbor_in, first_neighbor),
+                (first_bias_in, first_bias),
+                (second_self_in, second_self),
+                (second_neighbor_in, second_neighbor),
+                (second_bias_in, second_bias),
+                (labels_in, labels),
+                (train_mask_in, train_mask),
+            )
+        )
+    ]
+    for copy in small:
+        copy.start()
 
     perm = permutation()
     feature_copy.wait()
@@ -216,6 +251,7 @@
     to_down1 = send(own1, table1.at[pl.ds(2 * TILES, TILES)], halo1_send.at[1], halo1_recv.at[1], (z, down))
     to_up1.start()
     to_down1.start()
+    closing.extend([to_up1.wait_send, to_down1.wait_send])
 
     def send_x(group, source):
         return send(
@@ -254,39 +290,36 @@
         )
 
     loop(1, GROUPS, lambda o: send_x(around(o), z).start())
+    closing.append(lambda: loop(1, GROUPS, lambda o: send_x(around(o), z).wait_send()))
     x_own = pltpu.make_async_copy(
         table1.at[pl.ds(TILES + 8 * z, 8)], inputs1.at[z], local_sem.at[1]
     )
     x_own.start()
 
-    eye = (iota((256, 256), 0) == iota((256, 256), 1)).astype(F32).astype(BF16)
+    for copy in small:
+        copy.wait()
+
+    eye = (iota((256, 256), 0) == iota((256, 256), 1)).astype(F32)
     for part, weight in enumerate((first_self, first_neighbor)):
-        turned = lax.dot_general(eye, weight[...], NT_DIMS, preferred_element_type=F32)
+        turned = lax.dot_general(eye.astype(BF16), weight[...], NT_DIMS, preferred_element_type=F32)
         w1[:, LANES * part : LANES * (part + 1)] = turned.astype(BF16)
     pick = (iota((CLS_PAD, CLS), 0) == iota((CLS_PAD, CLS), 1)).astype(F32)
     for part, weight in enumerate((second_self, second_neighbor)):
-        turned = lax.dot_general(pick.astype(BF16), weight[...], NT_DIMS, preferred_element_type=F32)
-        w2[:, 256 * part : 256 * (part + 1)] = turned.astype(BF16)
-    column1 = jnp.sum(
-        jnp.where(iota((256, 256), 0) == iota((256, 256), 1), first_bias[...], 0.0),
-        axis=1,
-        keepdims=True,
-    )
+        padded = jnp.dot(pick.astype(BF16), weight[...], preferred_element_type=F32)
+        w2[:, 256 * part : 256 * (part + 1)] = padded.astype(BF16)
+    column1 = jnp.sum(jnp.where(eye > 0.5, first_bias[...], 0.0), axis=1, keepdims=True)
     b1[...] = jnp.broadcast_to(column1, (256, LANES))
     column2 = jnp.sum(jnp.where(pick > 0.5, second_bias[...], 0.0), axis=1, keepdims=True)
     column2 = jnp.where(iota((CLS_PAD, 1), 0) < CLS, column2, -1e30)
     b2[...] = jnp.broadcast_to(column2, (CLS_PAD, LANES))
-    both = jnp.where(
-        iota((16, GROUP), 0) < 8,
-        jnp.broadcast_to(labels[...].astype(F32), (16, GROUP)),
-        jnp.broadcast_to(train_mask[...].astype(F32), (16, GROUP)),
-    ).astype(BF16)
-    for u in range(8):
-        span = slice(LANES * u, LANES * (u + 1))
-        class_mask[:, span] = jnp.dot(both[:, span], perm, preferred_element_type=F32)
 
     loop(0, 16, lambda r: bit_copy(r).wait())
-    loop(0, TILES, lambda t: unpack_row_tile(t, count_ref, bits, adj))
+
+    def unpack_some(i):
+        for u in range(4):
+            unpack_row_tile(i * 4 + u, count_ref, bits, adj)
+
+    loop(0, TILES // 4, unpack_some)
 
     to_up1.wait_recv()
     to_down1.wait_recv()
@@ -301,13 +334,15 @@
 
     def first_group(o):
         group = around(o)
-        loop(0, 8, lambda u: first_tile(group * 8 + u))
+        for u in range(8):
+            first_tile(group * 8 + u)
 
         @pl.when(o < GROUPS)
         def _():
             send_m(group, z).start()
 
     loop(1, GROUPS + 1, first_group)
+    closing.append(lambda: loop(1, GROUPS, lambda o: send_m(around(o), z).wait_send()))
     m_own = pltpu.make_async_copy(
         stage1.at[pl.ds(8 * z, 8)], inputs1.at[8 + z], local_sem.at[2]
     )
@@ -326,6 +361,7 @@
 
     loop(0, 8, first_dense)
     loop(1, GROUPS, lambda o: send_h(around(o), z).start())
+    closing.append(lambda: loop(1, GROUPS, lambda o: send_h(around(o), z).wait_send()))
     table2[pl.ds(TILES + 8 * z, 8)] = parts1[z]
 
     def halo2(group, side, device):
@@ -343,6 +379,12 @@
 
     forward(z)
 
+    def restore(u):
+        moved = lax.dot_general(hidden[:, lanes(u)], perm, NT_DIMS, preferred_element_type=F32)
+        hidden_true[:, lanes(u)] = moved.astype(BF16)
+
+    loop(0, 8, restore)
+
     def pass_on(o):
         group = around(o)
         send_h(z, group).wait_recv()
@@ -350,6 +392,11 @@
 
     loop(1, GROUPS, pass_on)
 
+    def halo2_left(group):
+        halo2(group, 0, up).wait_send()
+        halo2(group, 1, down).wait_send()
+
+    closing.append(lambda: loop(0, GROUPS, halo2_left))
     def halo2_arrived(group):
         halo2(group, 0, up).wait_recv()
         halo2(group, 1, down).wait_recv()
@@ -363,30 +410,34 @@
 
     def second_group(o):
         group = around(o)
-        loop(0, 8, lambda u: second_tile(group * 8 + u))
+        for u in range(8):
+            second_tile(group * 8 + u)
 
         @pl.when(o < GROUPS)
         def _():
             send_n(group, z).start()
 
     loop(1, GROUPS + 1, second_group)
+    closing.append(lambda: loop(1, GROUPS, lambda o: send_n(around(o), z).wait_send()))
     parts2[z] = stage2[pl.ds(8 * z, 8)]
     loop(1, GROUPS, lambda o: send_n(z, around(o)).wait_recv())
 
     def second_dense(u, loss):
         span = lanes(u)
-        mean2[:, span] = parts2[:, u].reshape(256, LANES)
+        moved = lax.dot_general(
+            parts2[:, u].reshape(256, LANES), perm, NT_DIMS, preferred_element_type=F32
+        )
+        mean2[:, span] = moved.astype(BF16)
         score = (
-            jnp.dot(w2[:, :256], hidden[:, span], preferred_element_type=F32)
+            jnp.dot(w2[:, :256], hidden_true[:, span], preferred_element_type=F32)
             + jnp.dot(w2[:, 256:], mean2[:, span], preferred_element_type=F32)
             + b2[...]
         )
-        logits[:, span] = score
+        logits_rows[:, :, span] = score[:CLS].reshape(CLS, 1, LANES)
         exponent = jnp.exp(score)
         class_total = jnp.sum(exponent, axis=0, keepdims=True)
-        label = class_mask[0:1, span].astype(jnp.int32)
-        weight = class_mask[8:9, span]
-        chosen = iota((CLS_PAD, LANES), 0) == label
+        weight = train_mask[:, span].astype(F32)
+        chosen = iota((CLS_PAD, LANES), 0) == labels[:, span]
         own_score = jnp.sum(jnp.where(chosen, score, 0.0), axis=0, keepdims=True)
         slope = exponent * (1.0 / class_total) - jnp.where(chosen, 1.0, 0.0)
         grad[0:CLS_PAD, span] = (slope * (weight * scale)).astype(BF16)
@@ -394,35 +445,27 @@
 
     grad[CLS_PAD:256, :] = jnp.zeros((256 - CLS_PAD, GROUP), BF16)
     loss_lanes = lax.fori_loop(0, 8, second_dense, jnp.zeros((1, LANES), F32))
+    logits_copy = pltpu.make_async_copy(logits_rows, logits_out, local_sem.at[3])
+    logits_copy.start()
+    closing.append(logits_copy.wait)
+    for part, values in enumerate((hidden_true, mean2)):
+        product = lax.dot_general(grad[0:CLS_PAD], values[...], NT_DIMS, preferred_element_type=F32)
+        payload[2 * part * CLS_PAD : (2 * part + 1) * CLS_PAD] = product[:, :LANES]
+        payload[(2 * part + 1) * CLS_PAD : (2 * part + 2) * CLS_PAD] = product[:, LANES:]
+    bias = lax.dot_general(
+        jnp.ones((16, GROUP), BF16), grad[...], NT_DIMS, preferred_element_type=F32
+    )
+    payload[704:712] = bias[:8, :LANES]
+    payload[712:720] = bias[:8, LANES:]
     loss = jnp.sum(loss_lanes, axis=1, keepdims=True) * (scale * scale)
-    bias = jnp.sum(grad[...].astype(F32), axis=1, keepdims=True)
-    payload[0:256] = lax.dot_general(hidden[...], grad[0:128], NT_DIMS, preferred_element_type=F32)
-    payload[256:512] = lax.dot_general(mean2[...], grad[0:128], NT_DIMS, preferred_element_type=F32)
-    tail = grad[128:256]
-    tail_self = lax.dot_general(hidden[...], tail, NT_DIMS, preferred_element_type=F32)
-    tail_neighbor = lax.dot_general(mean2[...], tail, NT_DIMS, preferred_element_type=F32)
-    last = iota((256, LANES), 1) == 127
-    extra = jnp.where(iota((256, LANES), 0) == 200, loss, bias)
-    payload[512:768] = jnp.where(last, extra, tail_self + pltpu.roll(tail_neighbor, 64, 1))
+    payload[720:728] = jnp.broadcast_to(loss, (8, LANES))
+    payload[728:768] = jnp.zeros((40, LANES), F32)
 
     core_copy = send(
         payload.at[rows(1 - core, HALF), :], core_in, core_send.at[0], core_recv.at[0], (z, core_peer)
     )
     core_copy.start()
-
-    def turn(u):
-        turned = logits[:, lanes(u)].T
-        for low in range(8):
-            place = pl.ds(low, 16, stride=8)
-            turn_left[place, :] = turned[16 * low : 16 * low + 16, :LANES]
-            turn_right[place, : CLS_PAD - LANES] = turned[16 * low : 16 * low + 16, LANES:]
-        logits_rows[rows(u, LANES), :LANES] = turn_left[...]
-        logits_rows[rows(u, LANES), LANES:] = turn_right[:, : CLS - LANES]
-
-    loop(0, 8, turn)
-    logits_copy = pltpu.make_async_copy(logits_rows, logits_out.at[0], local_sem.at[3])
-    logits_copy.start()
-
+    closing.append(core_copy.wait_send)
     core_copy.wait_recv()
     half_sum[...] = payload[rows(core, HALF), :] + core_in[...]
 
@@ -436,6 +479,7 @@
         )
 
     loop(1, 16, lambda o: plane_copy(plane_peer(o), plane).start())
+    closing.append(lambda: loop(1, 16, lambda o: plane_copy(plane_peer(o), plane).wait_send()))
     plane_in[plane] = half_sum[rows(plane, PIECE), :]
     loop(1, 16, lambda o: plane_copy(plane, plane_peer(o)).wait_recv())
     line_in[z] = jnp.sum(plane_in[...], axis=0)
@@ -446,6 +490,7 @@
         )
 
     loop(1, GROUPS, lambda o: line_copy(around(o), z).start())
+    closing.append(lambda: loop(1, GROUPS, lambda o: line_copy(around(o), z).wait_send()))
     loop(1, GROUPS, lambda o: line_copy(z, around(o)).wait_recv())
     total[rows(core * 16 + plane, PIECE), :] = jnp.sum(line_in[...], axis=0)
 
@@ -454,6 +499,7 @@
         return send(part, part, back_send.at[target], back_recv.at[source], (z, target * 2 + core))
 
     loop(1, 16, lambda o: back_copy(plane_peer(o), plane).start())
+    closing.append(lambda: loop(1, 16, lambda o: back_copy(plane_peer(o), plane).wait_send()))
     loop(1, 16, lambda o: back_copy(plane, plane_peer(o)).wait_recv())
 
     def half_copy(which):
@@ -461,39 +507,47 @@
         return send(part, part, core_send.at[1], core_recv.at[1], (z, core_peer))
 
     half_copy(core).start()
+    closing.append(half_copy(core).wait_send)
     half_copy(1 - core).wait_recv()
-    result = pltpu.make_async_copy(total, total_out, local_sem.at[4])
-    result.start()
-
-    to_up1.wait_send()
-    to_down1.wait_send()
-
-    def left_line(o):
-        group = around(o)
-        send_x(group, z).wait_send()
-        send_m(group, z).wait_send()
-        send_h(group, z).wait_send()
-        send_n(group, z).wait_send()
-        line_copy(group, z).wait_send()
-
-    loop(1, GROUPS, left_line)
-
-    def left_halo(group):
-        halo2(group, 0, up).wait_send()
-        halo2(group, 1, down).wait_send()
-
-    loop(0, GROUPS, left_halo)
-
-    def left_plane(o):
-        target = plane_peer(o)
-        plane_copy(target, plane).wait_send()
-        back_copy(target, plane).wait_send()
-
-    loop(1, 16, left_plane)
-    core_copy.wait_send()
-    half_copy(core).wait_send()
-    logits_copy.wait()
-    result.wait()
+    for part, held in enumerate((grad_self, grad_neighbor)):
+        for side in range(2):
+            start = (2 * part + side) * CLS_PAD
+            held[:, LANES * side : LANES * (side + 1)] = total[start : start + CLS]
+    grad_bias[:, :LANES] = total[704:705]
+    grad_bias[:, LANES:] = total[712:713, : CLS - LANES]
+    loss_held[...] = total[720:721, :1]
+    results = (
+        (grad_self, grad_self_out),
+        (grad_neighbor, grad_neighbor_out),
+        (grad_bias, grad_bias_out),
+        (loss_held, loss_out),
+    )
+    for i, (src, dst) in enumerate(results):
+        copy = pltpu.make_async_copy(src, dst, small_sem.at[i])
+        copy.start()
+        closing.append(copy.wait)
+
+    for wait in closing:
+        wait()
+
+
+def hand_over(*refs):
+    sources, targets, places, arrive, leave = refs[:5], refs[5:10], refs[10:15], refs[15], refs[16]
+    inward = [
+        pltpu.make_async_copy(src, place, arrive.at[i])
+        for i, (src, place) in enumerate(zip(sources, places))
+    ]
+    outward = [
+        pltpu.make_async_copy(place, dst, leave.at[i])
+        for i, (place, dst) in enumerate(zip(places, targets))
+    ]
+    for copy in inward:
+        copy.start()
+    for first, second in zip(inward, outward):
+        first.wait()
+        second.start()
+    for copy in outward:
+        copy.wait()
 
 
 def shards(
@@ -512,18 +566,34 @@
 ):
     node_total = features.shape[2] * lax.axis_size("node")
     dma = pltpu.SemaphoreType.DMA
-    vmem = pl.BlockSpec(memory_space=pltpu.VMEM)
-    smem = pl.BlockSpec(memory_space=pltpu.SMEM)
     anywhere = pl.BlockSpec(memory_space=pl.ANY)
-    logits, total = pl.pallas_call(
+    results = (
+        jax.ShapeDtypeStruct((CLS, 1, GROUP), F32),
+        jax.ShapeDtypeStruct((CLS, 256), F32),
+        jax.ShapeDtypeStruct((CLS, 256), F32),
+        jax.ShapeDtypeStruct((1, CLS), F32),
+        jax.ShapeDtypeStruct((1, 1), F32),
+    )
+    held = pl.pallas_call(
         functools.partial(kernel, 1.0 / math.sqrt(node_total)),
-        out_shape=(
-            jax.ShapeDtypeStruct((1, GROUP, CLS), F32),
-            jax.ShapeDtypeStruct((2 * HALF, LANES), F32),
-        ),
-        in_specs=[anywhere, smem, smem, anywhere] + [vmem] * 8,
-        out_specs=(anywhere, anywhere),
+        out_shape=results,
+        in_specs=[anywhere] * 12,
+        out_specs=(anywhere,) * 5,
         scratch_shapes=[
+            pltpu.SMEM((SLOTS, TILES), jnp.int32),
+            pltpu.SMEM((1, TILES), jnp.int32),
+            pltpu.VMEM((1, GROUP), jnp.int32),
+            pltpu.VMEM((1, GROUP), jnp.int32),
+            pltpu.VMEM((LANES, 256), BF16),
+            pltpu.VMEM((LANES, 256), BF16),
+            pltpu.VMEM((1, 256), F32),
+            pltpu.VMEM((CLS, 256), BF16),
+            pltpu.VMEM((CLS, 256), BF16),
+            pltpu.VMEM((1, CLS), F32),
+            pltpu.VMEM((CLS, 256), F32),
+            pltpu.VMEM((CLS, 256), F32),
+            pltpu.VMEM((1, CLS), F32),
+            pltpu.VMEM((1, 1), F32),
             pltpu.VMEM((16, BLOCK), BF16),
             pltpu.VMEM((TILES, 128, LANES), jnp.int32),
             pltpu.VMEM((TILES, LANES, SLOTS * LANES), BF16),
@@ -537,15 +607,12 @@
             pltpu.VMEM((256, GROUP), BF16),
             pltpu.VMEM((256, GROUP), BF16),
             pltpu.VMEM((TILES, 8, LANES), F32),
+            pltpu.VMEM((256, GROUP), BF16),
             pltpu.VMEM((256, 256), BF16),
             pltpu.VMEM((CLS_PAD, 512), BF16),
             pltpu.VMEM((256, LANES), F32),
             pltpu.VMEM((CLS_PAD, LANES), F32),
-            pltpu.VMEM((16, GROUP), F32),
-            pltpu.VMEM((CLS_PAD, GROUP), F32),
-            pltpu.VMEM((GROUP, CLS), F32),
-            pltpu.VMEM((LANES, LANES), F32),
-            pltpu.VMEM((LANES, LANES), F32),
+            pltpu.VMEM((CLS, 1, GROUP), F32),
             pltpu.VMEM((256, GROUP), BF16),
             pltpu.VMEM((2 * HALF, LANES), F32),
             pltpu.VMEM((HALF, LANES), F32),
@@ -554,7 +621,8 @@
             pltpu.VMEM((GROUPS, PIECE, LANES), F32),
             pltpu.VMEM((2 * HALF, LANES), F32),
             dma((16,)),
-            dma((5,)),
+            dma((10,)),
+            dma((4,)),
             dma((2,)),
             dma((2,)),
             dma((GROUPS,)),
@@ -577,26 +645,32 @@
             dma((16,)),
         ],
         compiler_params=pltpu.CompilerParams(
-            collective_id=0, has_side_effects=True, vmem_limit_bytes=52 * 1024 * 1024
+            collective_id=0, has_side_effects=True, vmem_limit_bytes=62 * 1024 * 1024
         ),
     )(
         features,
-        tile_columns[0],
+        tile_bits,
+        tile_columns[0].T,
         tile_count,
-        tile_bits,
         labels,
         train_mask,
         first_self,
         first_neighbor,
         first_bias[None],
-        second_self,
-        second_neighbor,
+        second_self.T,
+        second_neighbor.T,
         second_bias[None],
     )
-    tail = total[512:]
-    grad_self = jnp.concatenate([total[:256], tail[:, : CLS - 128]], axis=1)
-    grad_neighbor = jnp.concatenate([total[256:512], tail[:, 64 : CLS - 64]], axis=1)
-    return (logits, tail[200, 127], grad_self, grad_neighbor, tail[:CLS, 127])
+    logits, grad_self, grad_neighbor, grad_bias, loss = pl.pallas_call(
+        hand_over,
+        out_shape=results,
+        in_specs=[anywhere] * 5,
+        out_specs=(anywhere,) * 5,
+        scratch_shapes=[pltpu.VMEM(r.shape, F32) for r in results] + [dma((5,)), dma((5,))],
+        compiler_params=pltpu.CompilerParams(vmem_limit_bytes=62 * 1024 * 1024),
+    )(*held)
+    logits = jnp.transpose(logits, (1, 2, 0))
+    return (logits, loss[0, 0], grad_self.T, grad_neighbor.T, grad_bias[0])
 
 
 def solution(mesh):

time: 133 us -> 103 us (0.77)
  Pallas kernels: 117 us -> 102 us
  local copies, waits for them, and re-layouts: 14.8 us -> 0 us
    pallas_call x1, Pallas kernels: 117 us -> 99.6 us  [shards(): pl.pallas_call(functools.partial(kernel, 1.0 / math.sqrt(node_total)), ou...]
    unnamed x22 -> x0, local copies, waits for them, and re-layouts: 13.4 us -> none
    pallas_call x0 -> x1, Pallas kernels: none -> 2.72 us  [shards(): pl.pallas_call(hand_over, out_shape=results, in_specs=[anywhere] * 5, out...]
    slice x4 -> x0, local copies, waits for them, and re-layouts: 1.44 us -> none  [the longest x2 1.33 us: shards(): return (logits, tail[200, 127], grad_self, grad_neighbor, tail[:CLS, 127])]
where the time goes in v2:
time: 103 us
  Pallas kernels  102 us (99%)
    pallas_call x1, Pallas kernels, shards(): pl.pallas_call(functools.partial(kernel, 1.0 / math.sqrt(node_total)), ou...  99.6 us
    pallas_call x1, Pallas kernels, shards(): pl.pallas_call(hand_over, out_shape=results, in_specs=[anywhere] * 5, out...  2.72 us

profile of v2, /device:TPU:1, one launch (start us, length us, event | category | flops | bytes accessed | tf_op | source)
XLA Modules:
  0.0 103.0 jit_solution(15898798227328658309)
XLA Ops:
  0.6 99.6 %shard_map.155 = (f32[172,1,1024]{2,1,0:T(1,128)}, f32[172,256]{1,0:T(8,128)}, f32[172,256]{1,0:T(8,128)}, f32[1,172]{1,0:T(1,128)}, f32[1,1]{1,0:T(1,128)}) custom-call(bf16[1,16,8192]{2,1,0:T(8,128)(2,1)} %features.1, s32[1,64,8,2048]{3,2,1,0:T(8,128)} %bit_words.1, s32[8,64]{1,0:T(8,128)} %bitcast.14, s32[1,64]{1,0:T(1,128)} %count_in.1, ...), custom_call_target="tpu_custom_call" | custom-call | tf_op jit(solution)/shard_map/pallas_call | solution.py:577
  100.3 2.7 %shard_map.156 = (f32[172,1,1024]{2,1,0:T(1,128)}, f32[172,256]{1,0:T(8,128)}, f32[172,256]{1,0:T(8,128)}, f32[1,172]{1,0:T(1,128)}, f32[1,1]{1,0:T(1,128)}) custom-call(f32[172,1,1024]{2,1,0:T(1,128)} %get-tuple-element.15.refs_0_, f32[172,256]{1,0:T(8,128)} %get-tuple-element.16.refs_1_, f32[172,256]{1,0:T(8,128)} %get-tuple-element.17.refs_2_, ...), custom_call_target="tpu_custom_call" | custom-call | tf_op jit(solution)/shard_map/pallas_call | solution.py:664

commit v3 on v2

--- a/solution.py
+++ b/solution.py
@@ -132,9 +132,9 @@
     parts1,
     parts2,
     hidden,
-    mean2,
     inv_degree,
-    hidden_true,
+    second_inputs,
+    own_scores,
     w1,
     w2,
     b1,
@@ -183,8 +183,16 @@
     def around(offset):
         return lax.rem(z + offset, GROUPS)
 
-    def plane_peer(offset):
-        return lax.rem(plane + offset, 16)
+    def far_first(i):
+        return around(4 + lax.div(i + 1, 2) * (1 - 2 * lax.rem(i, 2)))
+
+    plane_x, plane_y = lax.div(plane, 4), lax.rem(plane, 4)
+    plane_peers = [
+        lax.rem(plane_x + dx, 4) * 4 + lax.rem(plane_y + dy, 4)
+        for dx in (2, 1, 3, 0)
+        for dy in (2, 1, 3, 0)
+        if dx or dy
+    ]
 
     def send(src, dst, send_sem, recv_sem, device):
         return pltpu.make_async_remote_copy(
@@ -203,7 +211,8 @@
         pl.semaphore_signal(barrier, inc=1, device_id=device, device_id_type=MESH)
 
     loop(1, GROUPS, lambda o: greet((around(o), node)))
-    loop(1, 16, lambda o: greet((z, plane_peer(o) * 2 + core)))
+    for peer in plane_peers:
+        greet((z, peer * 2 + core))
     greet((z, up))
     greet((z, down))
 
@@ -239,11 +248,12 @@
     perm = permutation()
     feature_copy.wait()
 
-    def permute_features(t):
-        moved = jnp.dot(feats[:, lanes(t)], perm, preferred_element_type=F32)
-        table1[TILES + t] = moved.astype(BF16)
-
-    loop(0, TILES, permute_features)
+    def permute_features(i):
+        for u in range(16):
+            moved = jnp.dot(feats[:, lanes(16 * i + u)], perm, preferred_element_type=F32)
+            table1[TILES + 16 * i + u] = moved.astype(BF16)
+
+    loop(0, TILES // 16, permute_features)
     pl.semaphore_wait(barrier, 24)
 
     own1 = table1.at[pl.ds(TILES, TILES)]
@@ -262,39 +272,38 @@
             (group, node),
         )
 
-    def send_m(group, source):
+    def send_m(group, source, half):
         return send(
-            stage1.at[pl.ds(8 * group, 8)],
-            inputs1.at[8 + source],
-            m_send.at[group],
-            m_recv.at[source],
+            stage1.at[pl.ds(8 * group + 4 * half, 4)],
+            inputs1.at[8 + source, pl.ds(4 * half, 4)],
+            m_send.at[half, group],
+            m_recv.at[half, source],
             (group, node),
         )
 
-    def send_h(group, source):
+    def send_h(group, source, half):
         return send(
-            parts1.at[group],
-            table2.at[pl.ds(TILES + 8 * source, 8)],
-            h_send.at[group],
-            h_recv.at[source],
+            parts1.at[group, pl.ds(4 * half, 4)],
+            table2.at[pl.ds(TILES + 8 * source + 4 * half, 4)],
+            h_send.at[half, group],
+            h_recv.at[half, source],
             (group, node),
         )
 
-    def send_n(group, source):
+    def send_n(group, source, half):
         return send(
-            stage2.at[pl.ds(8 * group, 8)],
-            parts2.at[source],
-            n_send.at[group],
-            n_recv.at[source],
+            stage2.at[pl.ds(8 * group + 4 * half, 4)],
+            parts2.at[source, pl.ds(4 * half, 4)],
+            n_send.at[half, group],
+            n_recv.at[half, source],
             (group, node),
         )
 
-    loop(1, GROUPS, lambda o: send_x(around(o), z).start())
+    others = range(GROUPS - 1)
+    for i in others:
+        send_x(far_first(i), z).start()
     closing.append(lambda: loop(1, GROUPS, lambda o: send_x(around(o), z).wait_send()))
-    x_own = pltpu.make_async_copy(
-        table1.at[pl.ds(TILES + 8 * z, 8)], inputs1.at[z], local_sem.at[1]
-    )
-    x_own.start()
+    inputs1[z] = table1[pl.ds(TILES + 8 * z, 8)]
 
     for copy in small:
         copy.wait()
@@ -332,74 +341,92 @@
         inv_degree[t] = inverse
         stage1[t] = (sums[:16] * inverse[:1]).astype(BF16)
 
-    def first_group(o):
-        group = around(o)
-        for u in range(8):
-            first_tile(group * 8 + u)
-
-        @pl.when(o < GROUPS)
-        def _():
-            send_m(group, z).start()
-
-    loop(1, GROUPS + 1, first_group)
-    closing.append(lambda: loop(1, GROUPS, lambda o: send_m(around(o), z).wait_send()))
-    m_own = pltpu.make_async_copy(
-        stage1.at[pl.ds(8 * z, 8)], inputs1.at[8 + z], local_sem.at[2]
-    )
-    m_own.start()
-    x_own.wait()
-    m_own.wait()
+    def aggregate(tile, send_part, half):
+        def two_groups(i):
+            pair = [far_first(2 * i), far_first(2 * i + 1)]
+            for group in pair:
+                for u in range(4):
+                    tile(group * 8 + 4 * half + u)
+            send_part(pair[0], z, half).start()
+
+            @pl.when(i < 3)
+            def _():
+                send_part(pair[1], z, half).start()
+
+        loop(0, 4, two_groups)
+
+    def all_left(send_part):
+        def left(o):
+            for half in range(2):
+                send_part(around(o), z, half).wait_send()
+
+        closing.append(lambda: loop(1, GROUPS, left))
+
+    def all_arrived(send_part, half):
+        loop(1, GROUPS, lambda o: send_part(z, around(o), half).wait_recv())
+
+    for half in range(2):
+        aggregate(first_tile, send_m, half)
+    all_left(send_m)
+
+    def halo2(group, half, side, device):
+        return send(
+            table2.at[pl.ds(TILES + 8 * group + 4 * half, 4)],
+            table2.at[pl.ds(2 * TILES * side + 8 * group + 4 * half, 4)],
+            halo2_send.at[side, half, group],
+            halo2_recv.at[side, half, group],
+            (z, device),
+        )
+
+    def forward(group, half):
+        halo2(group, half, 0, up).start()
+        halo2(group, half, 1, down).start()
+
     loop(1, GROUPS, lambda o: send_x(z, around(o)).wait_recv())
-    loop(1, GROUPS, lambda o: send_m(z, around(o)).wait_recv())
-
-    def first_dense(u):
-        node_inputs = inputs1[:, u].reshape(256, LANES)
-        total1 = jnp.dot(w1[...], node_inputs, preferred_element_type=F32)
-        activated = jnp.maximum(total1 + b1[...], 0.0).astype(BF16)
-        hidden[:, lanes(u)] = activated
-        parts1[:, u] = activated.reshape(GROUPS, 32, LANES)
-
-    loop(0, 8, first_dense)
-    loop(1, GROUPS, lambda o: send_h(around(o), z).start())
-    closing.append(lambda: loop(1, GROUPS, lambda o: send_h(around(o), z).wait_send()))
-    table2[pl.ds(TILES + 8 * z, 8)] = parts1[z]
-
-    def halo2(group, side, device):
-        return send(
-            table2.at[pl.ds(TILES + 8 * group, 8)],
-            table2.at[pl.ds(2 * TILES * side + 8 * group, 8)],
-            halo2_send.at[side, group],
-            halo2_recv.at[side, group],
-            (z, device),
-        )
-
-    def forward(group):
-        halo2(group, 0, up).start()
-        halo2(group, 1, down).start()
-
-    forward(z)
-
-    def restore(u):
-        moved = lax.dot_general(hidden[:, lanes(u)], perm, NT_DIMS, preferred_element_type=F32)
-        hidden_true[:, lanes(u)] = moved.astype(BF16)
-
-    loop(0, 8, restore)
-
-    def pass_on(o):
-        group = around(o)
-        send_h(z, group).wait_recv()
-        forward(group)
-
-    loop(1, GROUPS, pass_on)
+    for half in range(2):
+        tiles = pl.ds(4 * half, 4)
+        inputs1[8 + z, tiles] = stage1[pl.ds(8 * z + 4 * half, 4)]
+        all_arrived(send_m, half)
+        for u in range(4 * half, 4 * half + 4):
+            node_inputs = inputs1[:, u].reshape(256, LANES)
+            total1 = jnp.dot(w1[...], node_inputs, preferred_element_type=F32)
+            activated = jnp.maximum(total1 + b1[...], 0.0).astype(BF16)
+            hidden[:, LANES * u : LANES * (u + 1)] = activated
+            parts1[:, u] = activated.reshape(GROUPS, 32, LANES)
+        for i in others:
+            send_h(far_first(i), z, half).start()
+        table2[pl.ds(TILES + 8 * z + 4 * half, 4)] = parts1[z, tiles]
+        forward(z, half)
+    all_left(send_h)
+
+    for u in range(8):
+        span = slice(LANES * u, LANES * (u + 1))
+        moved = lax.dot_general(hidden[:, span], perm, NT_DIMS, preferred_element_type=F32)
+        moved = moved.astype(BF16)
+        second_inputs[0, :, span] = moved
+        own_part = jnp.dot(w2[:, :256], moved, preferred_element_type=F32)
+        own_scores[:, span] = own_part + b2[...]
+
+    for half in range(2):
+
+        def pass_on(i):
+            group = far_first(i)
+            send_h(z, group, half).wait_recv()
+            forward(group, half)
+
+        loop(0, GROUPS - 1, pass_on)
 
     def halo2_left(group):
-        halo2(group, 0, up).wait_send()
-        halo2(group, 1, down).wait_send()
+        for half in range(2):
+            halo2(group, half, 0, up).wait_send()
+            halo2(group, half, 1, down).wait_send()
 
     closing.append(lambda: loop(0, GROUPS, halo2_left))
+
     def halo2_arrived(group):
-        halo2(group, 0, up).wait_recv()
-        halo2(group, 1, down).wait_recv()
+        for half in range(2):
+            halo2(group, half, 0, up).wait_recv()
+            halo2(group, half, 1, down).wait_recv()
 
     loop(0, GROUPS, halo2_arrived)
 
@@ -408,64 +435,71 @@
         sums = lax.dot_general(values, adj[t], NT_DIMS, preferred_element_type=F32)
         stage2[t] = (sums * inv_degree[t][:1]).astype(BF16)
 
-    def second_group(o):
-        group = around(o)
-        for u in range(8):
-            second_tile(group * 8 + u)
-
-        @pl.when(o < GROUPS)
-        def _():
-            send_n(group, z).start()
-
-    loop(1, GROUPS + 1, second_group)
-    closing.append(lambda: loop(1, GROUPS, lambda o: send_n(around(o), z).wait_send()))
-    parts2[z] = stage2[pl.ds(8 * z, 8)]
-    loop(1, GROUPS, lambda o: send_n(z, around(o)).wait_recv())
-
-    def second_dense(u, loss):
-        span = lanes(u)
-        moved = lax.dot_general(
-            parts2[:, u].reshape(256, LANES), perm, NT_DIMS, preferred_element_type=F32
-        )
-        mean2[:, span] = moved.astype(BF16)
-        score = (
-            jnp.dot(w2[:, :256], hidden_true[:, span], preferred_element_type=F32)
-            + jnp.dot(w2[:, 256:], mean2[:, span], preferred_element_type=F32)
-            + b2[...]
-        )
-        logits_rows[:, :, span] = score[:CLS].reshape(CLS, 1, LANES)
-        exponent = jnp.exp(score)
-        class_total = jnp.sum(exponent, axis=0, keepdims=True)
-        weight = train_mask[:, span].astype(F32)
-        chosen = iota((CLS_PAD, LANES), 0) == labels[:, span]
-        own_score = jnp.sum(jnp.where(chosen, score, 0.0), axis=0, keepdims=True)
-        slope = exponent * (1.0 / class_total) - jnp.where(chosen, 1.0, 0.0)
-        grad[0:CLS_PAD, span] = (slope * (weight * scale)).astype(BF16)
-        return loss + (jnp.log(class_total) - own_score) * weight
+    for half in range(2):
+        aggregate(second_tile, send_n, half)
+    all_left(send_n)
 
     grad[CLS_PAD:256, :] = jnp.zeros((256 - CLS_PAD, GROUP), BF16)
-    loss_lanes = lax.fori_loop(0, 8, second_dense, jnp.zeros((1, LANES), F32))
-    logits_copy = pltpu.make_async_copy(logits_rows, logits_out, local_sem.at[3])
-    logits_copy.start()
-    closing.append(logits_copy.wait)
-    for part, values in enumerate((hidden_true, mean2)):
-        product = lax.dot_general(grad[0:CLS_PAD], values[...], NT_DIMS, preferred_element_type=F32)
-        payload[2 * part * CLS_PAD : (2 * part + 1) * CLS_PAD] = product[:, :LANES]
-        payload[(2 * part + 1) * CLS_PAD : (2 * part + 2) * CLS_PAD] = product[:, LANES:]
+    loss_lanes = jnp.zeros((1, LANES), F32)
+
+    def gradient(part, half):
+        span = slice(512 * half, 512 * (half + 1))
+        product = lax.dot_general(
+            grad[0:CLS_PAD, span],
+            second_inputs[part, :, span],
+            NT_DIMS,
+            preferred_element_type=F32,
+        )
+        for side in range(2):
+            place = pl.ds(pl.multiple_of(HALF * part + CLS_PAD * side, 8), CLS_PAD)
+            values = product[:, LANES * side : LANES * (side + 1)]
+            payload[place] = values if half == 0 else payload[place] + values
+
+    for half in range(2):
+        parts2[z, pl.ds(4 * half, 4)] = stage2[pl.ds(8 * z + 4 * half, 4)]
+        all_arrived(send_n, half)
+        for u in range(4 * half, 4 * half + 4):
+            span = slice(LANES * u, LANES * (u + 1))
+            moved = lax.dot_general(
+                parts2[:, u].reshape(256, LANES), perm, NT_DIMS, preferred_element_type=F32
+            )
+            moved = moved.astype(BF16)
+            second_inputs[1, :, span] = moved
+            score = own_scores[:, span] + jnp.dot(w2[:, 256:], moved, preferred_element_type=F32)
+            logits_rows[:, :, span] = score[:CLS].reshape(CLS, 1, LANES)
+            exponent = jnp.exp(score)
+            class_total = jnp.sum(exponent, axis=0, keepdims=True)
+            weight = train_mask[:, span].astype(F32)
+            chosen = iota((CLS_PAD, LANES), 0) == labels[:, span]
+            own_score = jnp.sum(jnp.where(chosen, score, 0.0), axis=0, keepdims=True)
+            slope = exponent * (1.0 / class_total) - jnp.where(chosen, 1.0, 0.0)
+            grad[0:CLS_PAD, span] = (slope * (weight * scale)).astype(BF16)
+            loss_lanes = loss_lanes + (jnp.log(class_total) - own_score) * weight
+        if half == 0:
+            gradient(0, 0)
+            gradient(1, 0)
+
     bias = lax.dot_general(
         jnp.ones((16, GROUP), BF16), grad[...], NT_DIMS, preferred_element_type=F32
     )
-    payload[704:712] = bias[:8, :LANES]
-    payload[712:720] = bias[:8, LANES:]
     loss = jnp.sum(loss_lanes, axis=1, keepdims=True) * (scale * scale)
-    payload[720:728] = jnp.broadcast_to(loss, (8, LANES))
-    payload[728:768] = jnp.zeros((40, LANES), F32)
+    for part in range(2):
+        start = HALF * part + 2 * CLS_PAD
+        payload[start : start + 8] = bias[:8, :LANES]
+        payload[start + 8 : start + 16] = bias[:8, LANES:]
+        payload[start + 16 : start + 24] = jnp.broadcast_to(loss, (8, LANES))
+        payload[start + 24 : start + 32] = jnp.zeros((8, LANES), F32)
+    gradient(1 - core, 1)
 
     core_copy = send(
         payload.at[rows(1 - core, HALF), :], core_in, core_send.at[0], core_recv.at[0], (z, core_peer)
     )
     core_copy.start()
     closing.append(core_copy.wait_send)
+    gradient(core, 1)
+    logits_copy = pltpu.make_async_copy(logits_rows, logits_out, local_sem.at[3])
+    logits_copy.start()
+    closing.append(logits_copy.wait)
     core_copy.wait_recv()
     half_sum[...] = payload[rows(core, HALF), :] + core_in[...]
 
@@ -478,10 +512,12 @@
             (z, target * 2 + core),
         )
 
-    loop(1, 16, lambda o: plane_copy(plane_peer(o), plane).start())
-    closing.append(lambda: loop(1, 16, lambda o: plane_copy(plane_peer(o), plane).wait_send()))
+    for peer in plane_peers:
+        plane_copy(peer, plane).start()
+        closing.append(plane_copy(peer, plane).wait_send)
     plane_in[plane] = half_sum[rows(plane, PIECE), :]
-    loop(1, 16, lambda o: plane_copy(plane, plane_peer(o)).wait_recv())
+    for peer in plane_peers:
+        plane_copy(plane, peer).wait_recv()
     line_in[z] = jnp.sum(plane_in[...], axis=0)
 
     def line_copy(target, source):
@@ -489,7 +525,8 @@
             line_in.at[source], line_in.at[source], line_send.at[target], line_recv.at[source], (target, node)
         )
 
-    loop(1, GROUPS, lambda o: line_copy(around(o), z).start())
+    for i in others:
+        line_copy(far_first(i), z).start()
     closing.append(lambda: loop(1, GROUPS, lambda o: line_copy(around(o), z).wait_send()))
     loop(1, GROUPS, lambda o: line_copy(z, around(o)).wait_recv())
     total[rows(core * 16 + plane, PIECE), :] = jnp.sum(line_in[...], axis=0)
@@ -498,9 +535,11 @@
         part = total.at[rows(core * 16 + source, PIECE), :]
         return send(part, part, back_send.at[target], back_recv.at[source], (z, target * 2 + core))
 
-    loop(1, 16, lambda o: back_copy(plane_peer(o), plane).start())
-    closing.append(lambda: loop(1, 16, lambda o: back_copy(plane_peer(o), plane).wait_send()))
-    loop(1, 16, lambda o: back_copy(plane, plane_peer(o)).wait_recv())
+    for peer in plane_peers:
+        back_copy(peer, plane).start()
+        closing.append(back_copy(peer, plane).wait_send)
+    for peer in plane_peers:
+        back_copy(plane, peer).wait_recv()
 
     def half_copy(which):
         part = total.at[rows(which, HALF), :]
@@ -511,11 +550,11 @@
     half_copy(1 - core).wait_recv()
     for part, held in enumerate((grad_self, grad_neighbor)):
         for side in range(2):
-            start = (2 * part + side) * CLS_PAD
+            start = HALF * part + CLS_PAD * side
             held[:, LANES * side : LANES * (side + 1)] = total[start : start + CLS]
-    grad_bias[:, :LANES] = total[704:705]
-    grad_bias[:, LANES:] = total[712:713, : CLS - LANES]
-    loss_held[...] = total[720:721, :1]
+    grad_bias[:, :LANES] = total[352:353]
+    grad_bias[:, LANES:] = total[360:361, : CLS - LANES]
+    loss_held[...] = total[368:369, :1]
     results = (
         (grad_self, grad_self_out),
         (grad_neighbor, grad_neighbor_out),
@@ -605,9 +644,9 @@
             pltpu.VMEM((GROUPS, 8, 32, LANES), BF16),
             pltpu.VMEM((GROUPS, 8, 32, LANES), BF16),
             pltpu.VMEM((256, GROUP), BF16),
-            pltpu.VMEM((256, GROUP), BF16),
             pltpu.VMEM((TILES, 8, LANES), F32),
-            pltpu.VMEM((256, GROUP), BF16),
+            pltpu.VMEM((2, 256, GROUP), BF16),
+            pltpu.VMEM((CLS_PAD, GROUP), F32),
             pltpu.VMEM((256, 256), BF16),
             pltpu.VMEM((CLS_PAD, 512), BF16),
             pltpu.VMEM((256, LANES), F32),
@@ -627,14 +666,14 @@
             dma((2,)),
             dma((GROUPS,)),
             dma((GROUPS,)),
-            dma((GROUPS,)),
-            dma((GROUPS,)),
-            dma((GROUPS,)),
-            dma((GROUPS,)),
             dma((2, GROUPS)),
             dma((2, GROUPS)),
-            dma((GROUPS,)),
-            dma((GROUPS,)),
+            dma((2, GROUPS)),
+            dma((2, GROUPS)),
+            dma((2, 2, GROUPS)),
+            dma((2, 2, GROUPS)),
+            dma((2, GROUPS)),
+            dma((2, GROUPS)),
             dma((2,)),
             dma((2,)),
             dma((16,)),

time: 103 us -> 85.4 us (0.83)
  Pallas kernels: 102 us -> 84.7 us
    pallas_call x1, Pallas kernels: 99.6 us -> 82 us  [shards(): pl.pallas_call(functools.partial(kernel, 1.0 / math.sqrt(node_total)), ou...]
where the time goes in v3:
time: 85.4 us; the launch traced here: 85.3 us
  Pallas kernels  84.7 us (99%)
    pallas_call x1, Pallas kernels, shards(): pl.pallas_call(functools.partial(kernel, 1.0 / math.sqrt(node_total)), ou...  82 us
    pallas_call x1, Pallas kernels, shards(): pl.pallas_call(hand_over, out_shape=results, in_specs=[anywhere] * 5, out...  2.72 us

profile of v3, /device:TPU:1, one launch (start us, length us, event | category | flops | bytes accessed | tf_op | source)
XLA Modules:
  0.0 85.3 jit_solution(6568803969771872288)
XLA Ops:
  0.6 82.0 %shard_map.155 = (f32[172,1,1024]{2,1,0:T(1,128)}, f32[172,256]{1,0:T(8,128)}, f32[172,256]{1,0:T(8,128)}, f32[1,172]{1,0:T(1,128)}, f32[1,1]{1,0:T(1,128)}) custom-call(bf16[1,16,8192]{2,1,0:T(8,128)(2,1)} %features.1, s32[1,64,8,2048]{3,2,1,0:T(8,128)} %bit_words.1, s32[8,64]{1,0:T(8,128)} %bitcast.14, s32[1,64]{1,0:T(1,128)} %count_in.1, ...), custom_call_target="tpu_custom_call" | custom-call | tf_op jit(solution)/shard_map/pallas_call | solution.py:616
  82.6 2.7 %shard_map.156 = (f32[172,1,1024]{2,1,0:T(1,128)}, f32[172,256]{1,0:T(8,128)}, f32[172,256]{1,0:T(8,128)}, f32[1,172]{1,0:T(1,128)}, f32[1,1]{1,0:T(1,128)}) custom-call(f32[172,1,1024]{2,1,0:T(1,128)} %get-tuple-element.15.refs_0_, f32[172,256]{1,0:T(8,128)} %get-tuple-element.16.refs_1_, f32[172,256]{1,0:T(8,128)} %get-tuple-element.17.refs_2_, ...), custom_call_target="tpu_custom_call" | custom-call | tf_op jit(solution)/shard_map/pallas_call | solution.py:703

commit v4 on v3

--- a/solution.py
+++ b/solution.py
@@ -21,6 +21,8 @@
 CLS = 172
 CLS_PAD = 176
 PIECE = 24
+FIRST_PARTS = 2
+SECOND_PARTS = 2
 HALF = 384
 
 
@@ -73,9 +75,10 @@
         packed = exchange_bits(packed)
         for side in range(2):
             slot = 2 * pair + side
+            part = packed >> 16 if side else packed
             for low in range(8):
-                first = (packed >> (16 * side + low)) & 1
-                second = (packed >> (16 * side + 8 + low)) & 1
+                first = part & (1 << low)
+                second = part & (256 << low)
                 both = jnp.concatenate([first, second], axis=0).astype(F32).astype(BF16)
                 adj[t, 16 * low : 16 * low + 16, LANES * slot : LANES * (slot + 1)] = both
 
@@ -204,7 +207,15 @@
             device_id_type=MESH,
         )
 
+    def drain(ref, sem):
+        send(ref, ref, sem, sem, (z, up)).wait_recv()
+
     closing = []
+
+    def close():
+        while closing:
+            closing.pop(0)()
+
     barrier = pltpu.get_barrier_semaphore()
 
     def greet(device):
@@ -262,50 +273,113 @@
     to_up1.start()
     to_down1.start()
     closing.extend([to_up1.wait_send, to_down1.wait_send])
+    size1, size2 = 8 // FIRST_PARTS, 8 // SECOND_PARTS
 
     def send_x(group, source):
         return send(
             table1.at[pl.ds(TILES + 8 * group, 8)],
             inputs1.at[source],
-            x_send.at[group],
-            x_recv.at[source],
+            x_send,
+            x_recv,
             (group, node),
         )
 
-    def send_m(group, source, half):
+    def send_m(group, source, part):
         return send(
-            stage1.at[pl.ds(8 * group + 4 * half, 4)],
-            inputs1.at[8 + source, pl.ds(4 * half, 4)],
-            m_send.at[half, group],
-            m_recv.at[half, source],
+            stage1.at[pl.ds(8 * group + size1 * part, size1)],
+            inputs1.at[8 + source, pl.ds(size1 * part, size1)],
+            m_send,
+            m_recv.at[part],
             (group, node),
         )
 
-    def send_h(group, source, half):
+    def send_h(group, source, part):
         return send(
-            parts1.at[group, pl.ds(4 * half, 4)],
-            table2.at[pl.ds(TILES + 8 * source + 4 * half, 4)],
-            h_send.at[half, group],
-            h_recv.at[half, source],
+            parts1.at[group, pl.ds(size1 * part, size1)],
+            table2.at[pl.ds(TILES + 8 * source + size1 * part, size1)],
+            h_send,
+            h_recv.at[part, source],
             (group, node),
         )
 
-    def send_n(group, source, half):
+    def send_n(group, source, part):
         return send(
-            stage2.at[pl.ds(8 * group + 4 * half, 4)],
-            parts2.at[source, pl.ds(4 * half, 4)],
-            n_send.at[half, group],
-            n_recv.at[half, source],
+            stage2.at[pl.ds(8 * group + size2 * part, size2)],
+            parts2.at[source, pl.ds(size2 * part, size2)],
+            n_send,
+            n_recv.at[part],
             (group, node),
         )
 
     others = range(GROUPS - 1)
     for i in others:
         send_x(far_first(i), z).start()
-    closing.append(lambda: loop(1, GROUPS, lambda o: send_x(around(o), z).wait_send()))
+    closing.append(lambda: drain(inputs1.at[0:7], x_send))
     inputs1[z] = table1[pl.ds(TILES + 8 * z, 8)]
 
-    for copy in small:
+    for copy in small[:2]:
+        copy.wait()
+
+    loop(0, 16, lambda r: bit_copy(r).wait())
+
+    def unpack_some(i):
+        for u in range(4):
+            unpack_row_tile(i * 4 + u, count_ref, bits, adj)
+
+    loop(0, TILES // 4, unpack_some)
+
+    to_up1.wait_recv()
+    to_down1.wait_recv()
+
+    place = iota((8, LANES), 1)
+    exponents = place // 16 + 8 * ((place // 8) % 2)
+    unscale = jnp.ones((8, LANES), F32)
+    for bit in range(4):
+        unscale = unscale * jnp.where((exponents >> bit) & 1 == 1, 0.5 ** (1 << bit), 1.0)
+
+    def first_tile(t):
+        values = picked_tiles(t, first_column, column_ref, table1)
+        stacked = jnp.concatenate([values, jnp.ones((16, SLOTS * LANES), BF16)], axis=0)
+        sums = lax.dot_general(stacked, adj[t], NT_DIMS, preferred_element_type=F32)
+        inverse = unscale / jnp.maximum(sums[16:24] * unscale, 1.0)
+        inv_degree[t] = inverse
+        stage1[t] = (sums[:16] * inverse[:1]).astype(BF16)
+
+    def aggregate(tile, send_part, part, size):
+        count = 8 // size
+
+        def some_groups(i):
+            groups = [far_first(count * i + k) for k in range(count)]
+            for group in groups:
+                for u in range(size):
+                    tile(group * 8 + size * part + u)
+            for group in groups[:-1]:
+                send_part(group, z, part).start()
+
+            @pl.when(i < size - 1)
+            def _():
+                send_part(groups[-1], z, part).start()
+
+        loop(0, size, some_groups)
+
+    for part in range(FIRST_PARTS):
+        aggregate(first_tile, send_m, part, size1)
+    closing.append(lambda: drain(inputs1.at[8:15], m_send))
+
+    def halo2(group, part, side, device):
+        return send(
+            table2.at[pl.ds(TILES + 8 * group + size1 * part, size1)],
+            table2.at[pl.ds(2 * TILES * side + 8 * group + size1 * part, size1)],
+            halo2_send.at[side],
+            halo2_recv.at[side],
+            (z, device),
+        )
+
+    def forward(group, part):
+        halo2(group, part, 0, up).start()
+        halo2(group, part, 1, down).start()
+
+    for copy in small[2:]:
         copy.wait()
 
     eye = (iota((256, 256), 0) == iota((256, 256), 1)).astype(F32)
@@ -322,82 +396,22 @@
     column2 = jnp.where(iota((CLS_PAD, 1), 0) < CLS, column2, -1e30)
     b2[...] = jnp.broadcast_to(column2, (CLS_PAD, LANES))
 
-    loop(0, 16, lambda r: bit_copy(r).wait())
-
-    def unpack_some(i):
-        for u in range(4):
-            unpack_row_tile(i * 4 + u, count_ref, bits, adj)
-
-    loop(0, TILES // 4, unpack_some)
-
-    to_up1.wait_recv()
-    to_down1.wait_recv()
-
-    def first_tile(t):
-        values = picked_tiles(t, first_column, column_ref, table1)
-        stacked = jnp.concatenate([values, jnp.ones((16, SLOTS * LANES), BF16)], axis=0)
-        sums = lax.dot_general(stacked, adj[t], NT_DIMS, preferred_element_type=F32)
-        inverse = 1.0 / jnp.maximum(sums[16:24], 1.0)
-        inv_degree[t] = inverse
-        stage1[t] = (sums[:16] * inverse[:1]).astype(BF16)
-
-    def aggregate(tile, send_part, half):
-        def two_groups(i):
-            pair = [far_first(2 * i), far_first(2 * i + 1)]
-            for group in pair:
-                for u in range(4):
-                    tile(group * 8 + 4 * half + u)
-            send_part(pair[0], z, half).start()
-
-            @pl.when(i < 3)
-            def _():
-                send_part(pair[1], z, half).start()
-
-        loop(0, 4, two_groups)
-
-    def all_left(send_part):
-        def left(o):
-            for half in range(2):
-                send_part(around(o), z, half).wait_send()
-
-        closing.append(lambda: loop(1, GROUPS, left))
-
-    def all_arrived(send_part, half):
-        loop(1, GROUPS, lambda o: send_part(z, around(o), half).wait_recv())
-
-    for half in range(2):
-        aggregate(first_tile, send_m, half)
-    all_left(send_m)
-
-    def halo2(group, half, side, device):
-        return send(
-            table2.at[pl.ds(TILES + 8 * group + 4 * half, 4)],
-            table2.at[pl.ds(2 * TILES * side + 8 * group + 4 * half, 4)],
-            halo2_send.at[side, half, group],
-            halo2_recv.at[side, half, group],
-            (z, device),
-        )
-
-    def forward(group, half):
-        halo2(group, half, 0, up).start()
-        halo2(group, half, 1, down).start()
-
-    loop(1, GROUPS, lambda o: send_x(z, around(o)).wait_recv())
-    for half in range(2):
-        tiles = pl.ds(4 * half, 4)
-        inputs1[8 + z, tiles] = stage1[pl.ds(8 * z + 4 * half, 4)]
-        all_arrived(send_m, half)
-        for u in range(4 * half, 4 * half + 4):
+    drain(inputs1.at[0:7], x_recv)
+    for part in range(FIRST_PARTS):
+        tiles = pl.ds(size1 * part, size1)
+        inputs1[8 + z, tiles] = stage1[pl.ds(8 * z + size1 * part, size1)]
+        drain(inputs1.at[8:15, tiles], m_recv.at[part])
+        for u in range(size1 * part, size1 * (part + 1)):
             node_inputs = inputs1[:, u].reshape(256, LANES)
             total1 = jnp.dot(w1[...], node_inputs, preferred_element_type=F32)
             activated = jnp.maximum(total1 + b1[...], 0.0).astype(BF16)
             hidden[:, LANES * u : LANES * (u + 1)] = activated
             parts1[:, u] = activated.reshape(GROUPS, 32, LANES)
         for i in others:
-            send_h(far_first(i), z, half).start()
-        table2[pl.ds(TILES + 8 * z + 4 * half, 4)] = parts1[z, tiles]
-        forward(z, half)
-    all_left(send_h)
+            send_h(far_first(i), z, part).start()
+        table2[pl.ds(TILES + 8 * z + size1 * part, size1)] = parts1[z, tiles]
+        forward(z, part)
+    closing.append(lambda: drain(parts1.at[0:7], h_send))
 
     for u in range(8):
         span = slice(LANES * u, LANES * (u + 1))
@@ -407,37 +421,28 @@
         own_part = jnp.dot(w2[:, :256], moved, preferred_element_type=F32)
         own_scores[:, span] = own_part + b2[...]
 
-    for half in range(2):
+    for part in range(FIRST_PARTS):
 
         def pass_on(i):
             group = far_first(i)
-            send_h(z, group, half).wait_recv()
-            forward(group, half)
+            send_h(z, group, part).wait_recv()
+            forward(group, part)
 
         loop(0, GROUPS - 1, pass_on)
 
-    def halo2_left(group):
-        for half in range(2):
-            halo2(group, half, 0, up).wait_send()
-            halo2(group, half, 1, down).wait_send()
-
-    closing.append(lambda: loop(0, GROUPS, halo2_left))
-
-    def halo2_arrived(group):
-        for half in range(2):
-            halo2(group, half, 0, up).wait_recv()
-            halo2(group, half, 1, down).wait_recv()
-
-    loop(0, GROUPS, halo2_arrived)
+    for side in range(2):
+        block = table2.at[pl.ds(2 * TILES * side, TILES)]
+        closing.append(functools.partial(drain, block, halo2_send.at[side]))
+        drain(block, halo2_recv.at[side])
 
     def second_tile(t):
         values = picked_tiles(t, first_column, column_ref, table2)
         sums = lax.dot_general(values, adj[t], NT_DIMS, preferred_element_type=F32)
         stage2[t] = (sums * inv_degree[t][:1]).astype(BF16)
 
-    for half in range(2):
-        aggregate(second_tile, send_n, half)
-    all_left(send_n)
+    for part in range(SECOND_PARTS):
+        aggregate(second_tile, send_n, part, size2)
+    closing.append(lambda: drain(parts2.at[0:7], n_send))
 
     grad[CLS_PAD:256, :] = jnp.zeros((256 - CLS_PAD, GROUP), BF16)
     loss_lanes = jnp.zeros((1, LANES), F32)
@@ -457,7 +462,7 @@
 
     for half in range(2):
         parts2[z, pl.ds(4 * half, 4)] = stage2[pl.ds(8 * z + 4 * half, 4)]
-        all_arrived(send_n, half)
+        drain(parts2.at[0:7, pl.ds(4 * half, 4)], n_recv.at[half])
         for u in range(4 * half, 4 * half + 4):
             span = slice(LANES * u, LANES * (u + 1))
             moved = lax.dot_general(
@@ -507,39 +512,41 @@
         return send(
             half_sum.at[rows(target, PIECE), :],
             plane_in.at[source],
-            plane_send.at[target],
-            plane_recv.at[source],
+            plane_send,
+            plane_recv,
             (z, target * 2 + core),
         )
 
     for peer in plane_peers:
         plane_copy(peer, plane).start()
-        closing.append(plane_copy(peer, plane).wait_send)
+    close()
+    closing.append(lambda: drain(plane_in.at[0:15], plane_send))
     plane_in[plane] = half_sum[rows(plane, PIECE), :]
-    for peer in plane_peers:
-        plane_copy(plane, peer).wait_recv()
+    drain(plane_in.at[0:15], plane_recv)
     line_in[z] = jnp.sum(plane_in[...], axis=0)
 
     def line_copy(target, source):
         return send(
-            line_in.at[source], line_in.at[source], line_send.at[target], line_recv.at[source], (target, node)
+            line_in.at[source], line_in.at[source], line_send, line_recv, (target, node)
         )
 
     for i in others:
         line_copy(far_first(i), z).start()
-    closing.append(lambda: loop(1, GROUPS, lambda o: line_copy(around(o), z).wait_send()))
-    loop(1, GROUPS, lambda o: line_copy(z, around(o)).wait_recv())
+    close()
+    closing.append(lambda: drain(line_in.at[0:7], line_send))
+    drain(line_in.at[0:7], line_recv)
     total[rows(core * 16 + plane, PIECE), :] = jnp.sum(line_in[...], axis=0)
 
     def back_copy(target, source):
         part = total.at[rows(core * 16 + source, PIECE), :]
-        return send(part, part, back_send.at[target], back_recv.at[source], (z, target * 2 + core))
+        return send(part, part, back_send, back_recv, (z, target * 2 + core))
 
     for peer in plane_peers:
         back_copy(peer, plane).start()
-        closing.append(back_copy(peer, plane).wait_send)
-    for peer in plane_peers:
-        back_copy(plane, peer).wait_recv()
+    close()
+    pieces = total.at[0 : 15 * PIECE]
+    drain(pieces, back_recv)
+    closing.append(lambda: drain(pieces, back_send))
 
     def half_copy(which):
         part = total.at[rows(which, HALF), :]
@@ -566,20 +573,19 @@
         copy.start()
         closing.append(copy.wait)
 
-    for wait in closing:
-        wait()
+    close()
 
 
 def hand_over(*refs):
     sources, targets, places, arrive, leave = refs[:5], refs[5:10], refs[10:15], refs[15], refs[16]
-    inward = [
-        pltpu.make_async_copy(src, place, arrive.at[i])
-        for i, (src, place) in enumerate(zip(sources, places))
-    ]
-    outward = [
-        pltpu.make_async_copy(place, dst, leave.at[i])
-        for i, (place, dst) in enumerate(zip(places, targets))
-    ]
+    quarter = CLS // 4
+    cuts = [(k, slice(None)) for k in range(1, 5)]
+    cuts += [(0, slice(k * quarter, (k + 1) * quarter)) for k in range(4)]
+    inward, outward = [], []
+    for i, (k, cut) in enumerate(cuts):
+        place = places[k].at[cut]
+        inward.append(pltpu.make_async_copy(sources[k].at[cut], place, arrive.at[i]))
+        outward.append(pltpu.make_async_copy(place, targets[k].at[cut], leave.at[i]))
     for copy in inward:
         copy.start()
     for first, second in zip(inward, outward):
@@ -664,24 +670,24 @@
             dma((4,)),
             dma((2,)),
             dma((2,)),
-            dma((GROUPS,)),
-            dma((GROUPS,)),
-            dma((2, GROUPS)),
-            dma((2, GROUPS)),
-            dma((2, GROUPS)),
-            dma((2, GROUPS)),
-            dma((2, 2, GROUPS)),
-            dma((2, 2, GROUPS)),
-            dma((2, GROUPS)),
-            dma((2, GROUPS)),
+            dma(()),
+            dma(()),
+            dma(()),
+            dma((FIRST_PARTS,)),
+            dma(()),
+            dma((FIRST_PARTS, GROUPS)),
             dma((2,)),
             dma((2,)),
-            dma((16,)),
-            dma((16,)),
-            dma((GROUPS,)),
-            dma((GROUPS,)),
-            dma((16,)),
-            dma((16,)),
+            dma(()),
+            dma((SECOND_PARTS,)),
+            dma((2,)),
+            dma((2,)),
+            dma(()),
+            dma(()),
+            dma(()),
+            dma(()),
+            dma(()),
+            dma(()),
         ],
         compiler_params=pltpu.CompilerParams(
             collective_id=0, has_side_effects=True, vmem_limit_bytes=62 * 1024 * 1024
@@ -705,7 +711,7 @@
         out_shape=results,
         in_specs=[anywhere] * 5,
         out_specs=(anywhere,) * 5,
-        scratch_shapes=[pltpu.VMEM(r.shape, F32) for r in results] + [dma((5,)), dma((5,))],
+        scratch_shapes=[pltpu.VMEM(r.shape, F32) for r in results] + [dma((8,)), dma((8,))],
         compiler_params=pltpu.CompilerParams(vmem_limit_bytes=62 * 1024 * 1024),
     )(*held)
     logits = jnp.transpose(logits, (1, 2, 0))

time: 85.4 us -> 82.1 us (0.961)
  Pallas kernels: 84.7 us -> 81.4 us
    pallas_call x1, Pallas kernels: 82 us -> 78.7 us  [shards(): pl.pallas_call(functools.partial(kernel, 1.0 / math.sqrt(node_total)), ou...]
where the time goes in v4:
time: 82.1 us; the launch traced here: 82 us
  Pallas kernels  81.4 us (99%)
    pallas_call x1, Pallas kernels, shards(): pl.pallas_call(functools.partial(kernel, 1.0 / math.sqrt(node_total)), ou...  78.7 us
    pallas_call x1, Pallas kernels, shards(): pl.pallas_call(hand_over, out_shape=results, in_specs=[anywhere] * 5, out...  2.68 us

profile of v4, /device:TPU:1, one launch (start us, length us, event | category | flops | bytes accessed | tf_op | source)
XLA Modules:
  0.0 82.0 jit_solution(9337888235413707114)
XLA Ops:
  0.6 78.7 %shard_map.155 = (f32[172,1,1024]{2,1,0:T(1,128)}, f32[172,256]{1,0:T(8,128)}, f32[172,256]{1,0:T(8,128)}, f32[1,172]{1,0:T(1,128)}, f32[1,1]{1,0:T(1,128)}) custom-call(bf16[1,16,8192]{2,1,0:T(8,128)(2,1)} %features.1, s32[1,64,8,2048]{3,2,1,0:T(8,128)} %bit_words.1, s32[8,64]{1,0:T(8,128)} %bitcast.14, s32[1,64]{1,0:T(1,128)} %count_in.1, ...), custom_call_target="tpu_custom_call" | custom-call | tf_op jit(solution)/shard_map/pallas_call | solution.py:622
  79.3 2.7 %shard_map.156 = (f32[172,1,1024]{2,1,0:T(1,128)}, f32[172,256]{1,0:T(8,128)}, f32[172,256]{1,0:T(8,128)}, f32[1,172]{1,0:T(1,128)}, f32[1,1]{1,0:T(1,128)}) custom-call(f32[172,1,1024]{2,1,0:T(1,128)} %get-tuple-element.15.refs_0_, f32[172,256]{1,0:T(8,128)} %get-tuple-element.16.refs_1_, f32[172,256]{1,0:T(8,128)} %get-tuple-element.17.refs_2_, ...), custom_call_target="tpu_custom_call" | custom-call | tf_op jit(solution)/shard_map/pallas_call | solution.py:709

commit v5 on v4

--- a/solution.py
+++ b/solution.py
@@ -323,10 +323,10 @@
     loop(0, 16, lambda r: bit_copy(r).wait())
 
     def unpack_some(i):
-        for u in range(4):
-            unpack_row_tile(i * 4 + u, count_ref, bits, adj)
-
-    loop(0, TILES // 4, unpack_some)
+        for u in range(8):
+            unpack_row_tile(i * 8 + u, count_ref, bits, adj)
+
+    loop(0, TILES // 8, unpack_some)
 
     to_up1.wait_recv()
     to_down1.wait_recv()

time: 82.1 us -> 80.8 us (0.984)
  Pallas kernels: 81.4 us -> 80 us
    pallas_call x1, Pallas kernels: 78.7 us -> 77.3 us  [shards(): pl.pallas_call(functools.partial(kernel, 1.0 / math.sqrt(node_total)), ou...]
where the time goes in v5:
time: 80.8 us; the launch traced here: 80.6 us
  Pallas kernels  80 us (99%)
    pallas_call x1, Pallas kernels, shards(): pl.pallas_call(functools.partial(kernel, 1.0 / math.sqrt(node_total)), ou...  77.3 us
    pallas_call x1, Pallas kernels, shards(): pl.pallas_call(hand_over, out_shape=results, in_specs=[anywhere] * 5, out...  2.68 us

profile of v5, /device:TPU:1, one launch (start us, length us, event | category | flops | bytes accessed | tf_op | source)
XLA Modules:
  0.0 80.6 jit_solution(395308072038930517)
XLA Ops:
  0.6 77.3 %shard_map.155 = (f32[172,1,1024]{2,1,0:T(1,128)}, f32[172,256]{1,0:T(8,128)}, f32[172,256]{1,0:T(8,128)}, f32[1,172]{1,0:T(1,128)}, f32[1,1]{1,0:T(1,128)}) custom-call(bf16[1,16,8192]{2,1,0:T(8,128)(2,1)} %features.1, s32[1,64,8,2048]{3,2,1,0:T(8,128)} %bit_words.1, s32[8,64]{1,0:T(8,128)} %bitcast.14, s32[1,64]{1,0:T(1,128)} %count_in.1, ...), custom_call_target="tpu_custom_call" | custom-call | tf_op jit(solution)/shard_map/pallas_call | solution.py:622
  77.9 2.7 %shard_map.156 = (f32[172,1,1024]{2,1,0:T(1,128)}, f32[172,256]{1,0:T(8,128)}, f32[172,256]{1,0:T(8,128)}, f32[1,172]{1,0:T(1,128)}, f32[1,1]{1,0:T(1,128)}) custom-call(f32[172,1,1024]{2,1,0:T(1,128)} %get-tuple-element.15.refs_0_, f32[172,256]{1,0:T(8,128)} %get-tuple-element.16.refs_1_, f32[172,256]{1,0:T(8,128)} %get-tuple-element.17.refs_2_, ...), custom_call_target="tpu_custom_call" | custom-call | tf_op jit(solution)/shard_map/pallas_call | solution.py:709

commit v6 on v5

--- a/solution.py
+++ b/solution.py
@@ -323,10 +323,10 @@
     loop(0, 16, lambda r: bit_copy(r).wait())
 
     def unpack_some(i):
-        for u in range(8):
-            unpack_row_tile(i * 8 + u, count_ref, bits, adj)
-
-    loop(0, TILES // 8, unpack_some)
+        for u in range(16):
+            unpack_row_tile(i * 16 + u, count_ref, bits, adj)
+
+    loop(0, TILES // 16, unpack_some)
 
     to_up1.wait_recv()
     to_down1.wait_recv()

time: 80.8 us -> 89.1 us (1.10)
  Pallas kernels: 80 us -> 88.4 us
    pallas_call x1, Pallas kernels: 77.3 us -> 85.7 us  [shards(): pl.pallas_call(functools.partial(kernel, 1.0 / math.sqrt(node_total)), ou...]
where the time goes in v6:
time: 89.1 us; the launch traced here: 89 us
  Pallas kernels  88.4 us (99%)
    pallas_call x1, Pallas kernels, shards(): pl.pallas_call(functools.partial(kernel, 1.0 / math.sqrt(node_total)), ou...  85.7 us
    pallas_call x1, Pallas kernels, shards(): pl.pallas_call(hand_over, out_shape=results, in_specs=[anywhere] * 5, out...  2.68 us

profile of v6, /device:TPU:1, one launch (start us, length us, event | category | flops | bytes accessed | tf_op | source)
XLA Modules:
  0.0 89.0 jit_solution(7438349815942594944)
XLA Ops:
  0.6 85.7 %shard_map.155 = (f32[172,1,1024]{2,1,0:T(1,128)}, f32[172,256]{1,0:T(8,128)}, f32[172,256]{1,0:T(8,128)}, f32[1,172]{1,0:T(1,128)}, f32[1,1]{1,0:T(1,128)}) custom-call(bf16[1,16,8192]{2,1,0:T(8,128)(2,1)} %features.1, s32[1,64,8,2048]{3,2,1,0:T(8,128)} %bit_words.1, s32[8,64]{1,0:T(8,128)} %bitcast.14, s32[1,64]{1,0:T(1,128)} %count_in.1, ...), custom_call_target="tpu_custom_call" | custom-call | tf_op jit(solution)/shard_map/pallas_call | solution.py:622
  86.3 2.7 %shard_map.156 = (f32[172,1,1024]{2,1,0:T(1,128)}, f32[172,256]{1,0:T(8,128)}, f32[172,256]{1,0:T(8,128)}, f32[1,172]{1,0:T(1,128)}, f32[1,1]{1,0:T(1,128)}) custom-call(f32[172,1,1024]{2,1,0:T(1,128)} %get-tuple-element.15.refs_0_, f32[172,256]{1,0:T(8,128)} %get-tuple-element.16.refs_1_, f32[172,256]{1,0:T(8,128)} %get-tuple-element.17.refs_2_, ...), custom_call_target="tpu_custom_call" | custom-call | tf_op jit(solution)/shard_map/pallas_call | solution.py:709
